TPU v7x, 256 devices: a whole 4x4x8 slice. The times are simulated.
256 devices in a mesh: dp: 64 (over z, x, y_hi), ctx: 4 (over y_lo, core).
Axes of the slice: x: 4, y: 4 (y_hi: 2, y_lo: 2; y = y_hi * 2 + y_lo), z: 8, core: 2. Of those that a mesh axis runs over, the one named last changes fastest.
Arguments:
- queries: bfloat16 [192, 128, 576], P('dp', 'ctx'), may hold values from -25 to 25
- latent_cache: bfloat16 [192, 12800, 576], P('dp', 'ctx'), may hold values from -15 to 15
- lengths: int32 [192], P('dp'), may hold values from 2 to 12800, as said below
- value_up_matrix: bfloat16 [128, 512, 128], P('dp'), may hold values from -1.5 to 1.5
- out_weight: bfloat16 [16384, 7168], P('dp', 'ctx'), may hold values from -0.046875 to 0.046875
Outputs:
- layer_out: bfloat16 [192, 7168], P('dp', 'ctx')
Inputs may be any that keep to these rules, and one draw needn't show every extreme that they name: `lengths`: each row has 2 or more live positions; some row has all 12800.
All inputs are finite; a program needn't handle non-finite values.
Results may differ from a plain program's by a relative error of at most 0.022.
Values may be sent and summed in bfloat16 or wider, within the bound.
No kernel may reach another device: no remote copies, remote signals or barrier semaphores. Data moves between devices by JAX's collectives and lax.ppermute only.
A program may use at most 64 MiB of HBM per device.

v0:
```python
import jax
import jax.numpy as jnp
from jax import lax
from jax.sharding import PartitionSpec as P

ROPE = 64
QK = 128


def from_behind(block, axis, distance):
    devices = range(lax.axis_size(axis))
    route = [((i - distance) % len(devices), i) for i in devices]
    return lax.ppermute(block, axis, route)


def block_partial(query_rows, cache_rows, length_rows, positions, lat_width):
    score_scale = (QK + ROPE) ** (-0.5)
    scores = (
        jnp.einsum("nhw,ntw->nht", query_rows, cache_rows, preferred_element_type=jnp.float32)
        * score_scale
    )
    live_mask = (positions[None, :] < length_rows[:, None])[:, None, :]
    scores = jnp.where(live_mask, scores, -1e30)
    row_peak = jnp.max(scores, axis=2)
    weights = jnp.where(live_mask, jnp.exp(scores - row_peak[:, :, None]), 0.0)
    row_total = jnp.sum(weights, axis=2)
    accum_sum = jnp.einsum(
        "nht,ntk->nhk",
        weights.astype(jnp.bfloat16),
        cache_rows[:, :, :lat_width],
        preferred_element_type=jnp.float32,
    )
    return (row_peak, row_total, accum_sum)


def combine_state(first_state, second_state):
    peak_new = jnp.maximum(first_state[0], second_state[0])
    rescale_first = jnp.exp(first_state[0] - peak_new)
    factor_two = jnp.exp(second_state[0] - peak_new)
    updated_total = rescale_first * first_state[1] + factor_two * second_state[1]
    accum_new = (
        rescale_first[:, :, None] * first_state[2] + factor_two[:, :, None] * second_state[2]
    )
    return (peak_new, updated_total, accum_new)


def shards(queries, latent_cache, lengths, value_up_matrix, out_weight):
    row_count = queries.shape[0]
    block_heads = queries.shape[1]
    lat_width = value_up_matrix.shape[1]
    groups = lax.axis_size("ctx")
    context_position = lax.axis_index("ctx")
    shard_len = latent_cache.shape[1]
    positions = context_position * shard_len + lax.iota(jnp.int32, shard_len)
    carry_query = queries
    row_peak = jnp.full((row_count, block_heads), -1e30, jnp.float32)
    row_total = jnp.zeros((row_count, block_heads), jnp.float32)
    accum_sum = jnp.zeros((row_count, block_heads, lat_width), jnp.float32)
    for hop_index in range(groups):
        fresh = block_partial(carry_query, latent_cache, lengths, positions, lat_width)
        row_peak, row_total, accum_sum = combine_state((row_peak, row_total, accum_sum), fresh)
        carry_query, row_peak, row_total, accum_sum = (
            from_behind(carry_query, "ctx", 1),
            from_behind(row_peak.astype(jnp.bfloat16), "ctx", 1).astype(row_peak.dtype),
            from_behind(row_total.astype(jnp.bfloat16), "ctx", 1).astype(row_total.dtype),
            from_behind(accum_sum.astype(jnp.bfloat16), "ctx", 1).astype(accum_sum.dtype),
        )
    latent_result = (accum_sum / row_total[:, :, None]).astype(jnp.bfloat16)
    owned = value_up_matrix.shape[0]
    block_rows = lax.all_gather(latent_result, "ctx", axis=1, tiled=True)
    forwarded_partials = lax.all_to_all(block_rows, "dp", split_axis=1, concat_axis=0, tiled=True)
    head_result = jnp.einsum(
        "rod,odm->rom", forwarded_partials, value_up_matrix, preferred_element_type=jnp.float32
    ).astype(jnp.bfloat16)
    flat_heads = head_result.reshape(head_result.shape[0], owned * head_result.shape[2])
    return lax.psum_scatter(
        jnp.dot(flat_heads, out_weight, preferred_element_type=jnp.float32),
        "dp",
        scatter_dimension=0,
        tiled=True,
    ).astype(jnp.bfloat16)


def solution(mesh):
    return jax.shard_map(
        shards,
        mesh=mesh,
        in_specs=(
            P("dp", "ctx", None),
            P("dp", "ctx", None),
            P("dp"),
            P("dp", None, None),
            P("dp", "ctx"),
        ),
        out_specs=P("dp", "ctx"),
        check_vma=False,
    )
```

profile of v0, /device:TPU:8, one launch (start us, length us, event | category | flops | bytes accessed | tf_op | source)
XLA Modules:
  0.0 459.8 jit_solution(3057689444346426958)
XLA Ops:
  0.0 0.0 copy-start
  0.0 0.0 collective-permute-start.1
  0.0 0.8 broadcast_compare_fusion
  0.8 0.0 copy-start.1
  0.9 6.4 %fusion.79 = (f32[3,32]{1,0:T(4,128)S(1)}, f32[3,32,3200]{2,1,0:T(8,128)S(1)}) fusion(bf16[3,32,576]{2,1,0:T(8,128)(2,1)} %param.5, bf16[3,3200,576]{1,2,0:T(8,128)(2,1)} %param.6, pred[3,3200]{1,0:T(4,128)(4,1)S(1)} %broadcast_compare_fusion), kind=kOutput, calls=%fused_computation.88 | convolution fusion | flops 354815904 | bytes 12408576 | tf_op jit(solution)/shard_map/nhw,ntw->nht/dot_general | solution.py:19
  7.2 2.3 collective-permute-start
  9.5 0.0 collective-permute-done.1
  9.5 0.1 collective-permute-start.3
  9.6 0.0 copy-done.1
  9.6 2.0 fusion.80
  11.7 0.0 collective-permute-done
  11.7 0.9 collective-permute-start.2
  12.5 1.3 collective-permute-done.3
  13.8 2.0 fusion.78
  15.8 0.0 collective-permute-done.2
  15.8 0.1 collective-permute-start.4
  15.9 0.3 collective-permute-start.5
  16.2 3.0 fusion
  19.2 1.3 collective-permute-done.5
  20.5 2.0 fusion.77
  22.5 1.1 fusion.22
  23.7 0.1 collective-permute-start.10
  23.8 3.0 fusion.18
  26.8 3.0 fusion.6
  29.8 0.7 collective-permute-start.6
  30.5 0.0 collective-permute-done.10
  30.5 0.3 collective-permute-start.11
  30.9 3.0 collective-permute-done.6
  33.9 3.0 add_convert_fusion.2
  36.9 0.1 collective-permute-start.7
  37.0 0.0 collective-permute-done.11
  37.0 1.0 collective-permute-start.12
  38.0 3.0 collective-permute-done.7
  41.0 0.1 add_convert_fusion.1
  41.1 0.3 collective-permute-start.8
  41.4 0.0 collective-permute-done.4
  41.5 0.0 collective-permute-done.12
  41.5 4.0 collective-permute-done.8
  45.5 0.1 add_convert_fusion
  45.6 0.1 collective-permute-start.9
  45.7 1.0 collective-permute-start.13
  46.6 3.1 collective-permute-done.13
  49.7 0.0 collective-permute-done.9
  49.7 0.1 divide_convert_fusion
  49.8 0.0 copy-start.3
  49.9 6.1 %all_gather.3 = bf16[3,128,512]{2,1,0:T(8,128)(2,1)S(1)} all-gather(bf16[3,32,512]{2,1,0:T(8,128)(2,1)S(1)} %divide_convert_fusion), channel_id=1, replica_groups=mesh['dp'=64,'ctx'=4] {'ctx'}, dimensions={1}, use_global_device_ids=true | all-gather | bytes 491520 | tf_op jit(solution)/shard_map/all_gather | solution.py:70
  56.0 1.1 copy.13
  57.1 0.0 copy-start.2
  57.1 12.5 %all-to-all-start = ((bf16[3,128,512]{2,0,1:T(4,128)(2,1)}), bf16[3,128,512]{2,0,1:T(4,128)(2,1)S(1)}, u32[]{:S(2)}, u32[]{:S(2)}) async-start(bf16[3,128,512]{2,0,1:T(4,128)(2,1)} %copy.13), calls=%async_computation | async-start | bytes 1048576 | tf_op jit(solution)/shard_map/all_to_all | solution.py:71
  69.6 0.0 copy-done.3
  69.6 0.6 dynamic-slice
  70.9 18.6 %all-to-all-done = bf16[3,128,512]{2,0,1:T(4,128)(2,1)S(1)} async-done(((bf16[3,128,512]{2,0,1:T(4,128)(2,1)}), bf16[3,128,512]{2,0,1:T(4,128)(2,1)S(1)}, u32[]{:S(2)}, u32[]{:S(2)}) %all-to-all-start) | async-done | bytes 393248 | tf_op jit(solution)/shard_map/all_to_all | solution.py:71
  89.4 0.3 copy.14
  89.8 0.0 copy-done.2
  89.8 0.3 fusion.21
  90.0 0.0 copy-done
  90.0 0.4 fusion.47
  90.4 368.8 %all-reduce.2 = bf16[192,1792]{1,0:T(8,128)(2,1)S(1)} all-reduce(f32[192,1792]{1,0:T(8,128)S(1)} %fusion.47), channel_id=2, replica_groups=mesh['dp'=64,'ctx'=4] {'dp'}, use_global_device_ids=true, to_apply=%region_8.9.clone | all-reduce | flops 344064 | bytes 2064384
  459.2 0.6 dynamic-slice_convert_fusion
  (9 shorter events, 0.1 us)
Async XLA Ops:
  0.0 90.0 %copy-start = (bf16[256,1792]{1,0:T(8,128)(2,1)S(1)}, bf16[256,1792]{1,0:T(8,128)(2,1)}, u32[]{:S(2)}) copy-start(bf16[256,1792]{1,0:T(8,128)(2,1)} %param.9) | copy-start | bytes 2752516
  0.0 9.5 %collective-permute-start.1 = (bf16[3,32,576]{2,1,0:T(8,128)(2,1)}, bf16[3,32,576]{2,1,0:T(8,128)(2,1)S(1)}, u32[]{:S(2)}, u32[]{:S(2)}) collective-permute-start(bf16[3,32,576]{2,1,0:T(8,128)(2,1)} %param.5), channel_id=1, source_target_pairs={{3,0},{0,1},{1,2},{2,3},{7,4},{4,5},{5,6},{6,7},{11,8},{8,9},{9,10... | collective-permute-start | bytes 331784 | tf_op jit(solution)/shard_map/ppermute | solution.py:13
  0.8 8.8 %copy-start.1 = (bf16[3,3200,576]{1,2,0:T(8,128)(2,1)S(1)}, bf16[3,3200,576]{1,2,0:T(8,128)(2,1)}, u32[]{:S(2)}) copy-start(bf16[3,3200,576]{1,2,0:T(8,128)(2,1)} %param.6) | copy-start | bytes 33177604
  7.2 4.4 collective-permute-start
  9.5 4.3 collective-permute-start.3
  11.7 4.1 collective-permute-start.2
  15.8 25.6 %collective-permute-start.4 = (bf16[3,32]{1,0:T(4,128)(2,1)S(1)}, bf16[3,32]{1,0:T(4,128)(2,1)S(1)}, u32[]{:S(2)}, u32[]{:S(2)}) collective-permute-start(bf16[3,32]{1,0:T(4,128)(2,1)S(1)} %fusion.53), channel_id=1, source_target_pairs={{3,0},{0,1},{1,2},{2,3},{7,4},{4,5},{5,6},{6,7},{11,8},{8,9},{9,10... | collective-permute-start | bytes 584 | tf_op jit(solution)/shard_map/ppermute | solution.py:13
  15.9 4.6 collective-permute-start.5
  23.7 6.9 %collective-permute-start.10 = (bf16[3,32]{1,0:T(4,128)(2,1)S(1)}, bf16[3,32]{1,0:T(4,128)(2,1)S(1)}, u32[]{:S(2)}, u32[]{:S(2)}) collective-permute-start(bf16[3,32]{1,0:T(4,128)(2,1)S(1)} %get-tuple-element.18), channel_id=1, source_target_pairs={{3,0},{0,1},{1,2},{2,3},{7,4},{4,5},{5,6},{6,7},{11,8},{8,9},{9,10... | collective-permute-start | bytes 584 | tf_op jit(solution)/shard_map/ppermute | solution.py:13
  29.8 4.1 collective-permute-start.6
  30.5 6.5 %collective-permute-start.11 = (bf16[3,32]{1,0:T(4,128)(2,1)S(1)}, bf16[3,32]{1,0:T(4,128)(2,1)S(1)}, u32[]{:S(2)}, u32[]{:S(2)}) collective-permute-start(bf16[3,32]{1,0:T(4,128)(2,1)S(1)} %get-tuple-element.15), channel_id=1, source_target_pairs={{3,0},{0,1},{1,2},{2,3},{7,4},{4,5},{5,6},{6,7},{11,8},{8,9},{9,10... | collective-permute-start | bytes 584 | tf_op jit(solution)/shard_map/ppermute | solution.py:13
  36.9 4.1 collective-permute-start.7
  37.0 4.4 collective-permute-start.12
  41.1 4.3 collective-permute-start.8
  45.6 4.2 collective-permute-start.9
  45.7 4.1 collective-permute-start.13
  49.8 19.8 %copy-start.3 = (u32[256]{0:T(256)S(1)}, u32[256]{0:T(256)}, u32[]{:S(2)}) copy-start(u32[256]{0:T(256)} %constant.23) | copy-start | bytes 3076
  57.1 32.6 %copy-start.2 = (bf16[2,512,128]{2,1,0:T(8,128)(2,1)S(1)}, bf16[2,512,128]{2,1,0:T(8,128)(2,1)}, u32[]{:S(2)}) copy-start(bf16[2,512,128]{2,1,0:T(8,128)(2,1)} %param.8) | copy-start | bytes 786436
  57.1 32.3 %all-to-all-start = ((bf16[3,128,512]{2,0,1:T(4,128)(2,1)}), bf16[3,128,512]{2,0,1:T(4,128)(2,1)S(1)}, u32[]{:S(2)}, u32[]{:S(2)}) async-start(bf16[3,128,512]{2,0,1:T(4,128)(2,1)} %copy.13), calls=%async_computation | async-start | bytes 1048576 | tf_op jit(solution)/shard_map/all_to_all | solution.py:71
where the time goes:
time: 460 us
  blocking collectives  375 us (82%)
  waiting for transfers between devices  34.2 us (7%)
  matrix products  25.1 us (5%)
  starting transfers between devices  19.6 us (4%)
    unnamed x1, blocking collectives  369 us
    all_to_all x1, waiting for transfers between devices, shards(): lax.all_to_all(block_rows, 'dp', split_axis=1, concat_axis=0, tiled=True)  18.6 us
    ppermute x14, waiting for transfers between devices, from_behind(): return lax.ppermute(block, axis, route)  15.7 us
    all_to_all x1, starting transfers between devices, shards(): lax.all_to_all(block_rows, 'dp', split_axis=1, concat_axis=0, tiled=True)  12.5 us
    dot_general x4, matrix products, block_partial(): jnp.einsum('nhw,ntw->nht', query_rows, cache_rows, preferred_element_type...  12.4 us
    dot_general x4, matrix products, block_partial(): jnp.einsum('nht,ntk->nhk', weights.astype(jnp.bfloat16), cache_rows[:, :,...  12.1 us
  transfers between devices with their start and end apart: 15, of which 7 were waited for; matrix products, arithmetic and copies ran while one was open for 6% of the time, Pallas kernels for 0%

commit v1 on v0

v1 whole, which is shorter than its diff:
```python
import functools

import jax
import jax.numpy as jnp
import numpy as np
from jax import lax
from jax.experimental import pallas as pl
from jax.experimental.pallas import tpu as pltpu
from jax.sharding import Mesh, PartitionSpec as P

ROPE = 64
QK = 128
SCALE = (QK + ROPE) ** -0.5
DEAD = -1e30
DP = ("z", "x", "yh")
CTX = ("yl", "core")
STAT_ROWS = 16
VMEM = pl.BlockSpec(memory_space=pltpu.VMEM)
SMEM = pl.BlockSpec(memory_space=pltpu.SMEM)


def product(a, b, dim_a, dim_b):
    return lax.dot_general(
        a, b, (((dim_a,), (dim_b,)), ((), ())), preferred_element_type=jnp.float32
    )


def attend_kernel(rows, heads, lat, query_ref, cache_ref, length_ref, out_ref, stat_ref):
    row = pl.program_id(0)
    scores = product(query_ref[0], cache_ref[0], 1, 0) * SCALE
    positions = lax.broadcasted_iota(jnp.int32, scores.shape, 1)
    scores = jnp.where(positions < length_ref[row], scores, DEAD)
    peak = jnp.max(scores, axis=1, keepdims=True)
    weights = jnp.exp(scores - peak)
    total = jnp.sum(weights, axis=1, keepdims=True)
    mixed = product(weights.astype(jnp.bfloat16), cache_ref[0, :lat], 1, 1)
    mixed = (mixed / total).astype(jnp.bfloat16)
    quarters = out_ref.shape[0]
    width = lat // quarters
    place = pl.ds(pl.multiple_of(row * heads, heads), heads)
    for k in range(quarters):
        out_ref[k, place, :] = mixed[:, k * width : (k + 1) * width]
    logsum = jnp.broadcast_to(peak + jnp.log(total), (heads, heads)).T[0:1]
    high = logsum.astype(jnp.bfloat16).astype(jnp.float32)
    middle = (logsum - high).astype(jnp.bfloat16).astype(jnp.float32)
    low = logsum - high - middle

    @pl.when(row == 0)
    def _():
        stat_ref[...] = jnp.zeros_like(stat_ref)

    stat_ref[pl.ds(3 * row, 1), :] = high
    stat_ref[pl.ds(3 * row + 1, 1), :] = middle
    stat_ref[pl.ds(3 * row + 2, 1), :] = low

    @pl.when(row == rows - 1)
    def _():
        for k in range(quarters):
            out_ref[k, rows * heads :, :] = stat_ref[...].astype(jnp.bfloat16)


def attend(queries, cache, lengths, lat, quarters):
    rows, heads, width = queries.shape
    span = cache.shape[2]
    shape = (quarters, rows * heads + STAT_ROWS, lat // quarters)
    return pl.pallas_call(
        functools.partial(attend_kernel, rows, heads, lat),
        grid=(rows,),
        in_specs=[
            pl.BlockSpec((1, heads, width), lambda i: (i, 0, 0)),
            pl.BlockSpec((1, width, span), lambda i: (i, 0, 0)),
            SMEM,
        ],
        out_specs=pl.BlockSpec(shape, lambda i: (0, 0, 0)),
        out_shape=jax.ShapeDtypeStruct(shape, jnp.bfloat16),
        scratch_shapes=[pltpu.VMEM((STAT_ROWS, heads), jnp.float32)],
        compiler_params=pltpu.CompilerParams(vmem_limit_bytes=48 << 20),
        name="attend",
    )(queries, cache, lengths)


def combine_kernel(rows, heads, part_ref, order_ref, out_ref):
    parts = part_ref.shape[0]
    stats = [part_ref[c, rows * heads :, :].astype(jnp.float32) for c in range(parts)]
    shares = []
    for row in range(rows):
        logsums = [s[3 * row : 3 * row + 1] + s[3 * row + 1 : 3 * row + 2] + s[3 * row + 2 : 3 * row + 3] for s in stats]
        peak = functools.reduce(jnp.maximum, logsums)
        factors = [jnp.exp(v - peak) for v in logsums]
        total = functools.reduce(jnp.add, factors)
        shares += [f / total for f in factors]
    shares.append(jnp.zeros((heads - len(shares), heads), jnp.float32))
    shares = jnp.concatenate(shares, axis=0).T
    merged = []
    for row in range(rows):
        total = None
        for c in range(parts):
            column = row * parts + c
            term = shares[:, column : column + 1] * part_ref[c, row * heads : (row + 1) * heads, :].astype(jnp.float32)
            total = term if total is None else total + term
        merged.append(total.astype(jnp.bfloat16))
    merged = jnp.concatenate(merged, axis=0)
    out_ref[...] = product(order_ref[...], merged, 1, 0).astype(jnp.bfloat16)


def combine(parts, order, rows, heads):
    return pl.pallas_call(
        functools.partial(combine_kernel, rows, heads),
        in_specs=[VMEM, VMEM],
        out_specs=VMEM,
        out_shape=jax.ShapeDtypeStruct((order.shape[0], parts.shape[2]), jnp.bfloat16),
        compiler_params=pltpu.CompilerParams(vmem_limit_bytes=32 << 20),
        name="combine",
    )(parts, order)


def project_kernel(owned, latent_ref, up_ref, select_ref, weight_ref, out_ref):
    latents = jnp.concatenate([latent_ref[k] for k in range(latent_ref.shape[0])], axis=1)
    ups = jnp.concatenate([up_ref[o] for o in range(owned)], axis=1)
    heads_out = product(latents, ups, 1, 0)
    slot = lax.broadcasted_iota(jnp.int32, heads_out.shape, 0) % 8
    column = lax.broadcasted_iota(jnp.int32, heads_out.shape, 1)
    mine = (slot // 4) == (column // up_ref.shape[2])
    heads_out = jnp.where(mine, heads_out, 0.0).astype(jnp.bfloat16)
    flat = product(select_ref[...], heads_out, 1, 0).astype(jnp.bfloat16)
    out_ref[...] = product(flat, weight_ref[...], 1, 0).astype(jnp.bfloat16)


def project(latents, ups, select, weight):
    return pl.pallas_call(
        functools.partial(project_kernel, ups.shape[0]),
        in_specs=[VMEM] * 4,
        out_specs=VMEM,
        out_shape=jax.ShapeDtypeStruct((select.shape[0], weight.shape[1]), jnp.bfloat16),
        compiler_params=pltpu.CompilerParams(vmem_limit_bytes=32 << 20),
        name="project",
    )(latents, ups, select, weight)


def shards(queries, cache, lengths, ups, weight):
    rows = queries.shape[0]
    owned, lat, _ = ups.shape
    z, x, yh = (lax.axis_size(a) for a in DP)
    near = x * yh
    owners = z * near
    groups = lax.axis_size(CTX[0]) * lax.axis_size(CTX[1])
    heads = queries.shape[1] * groups
    span = cache.shape[1]
    context = lax.axis_index(CTX)

    all_queries = lax.all_gather(queries, CTX, axis=1, tiled=True)
    parts = attend(all_queries, jnp.swapaxes(cache, 1, 2), lengths - context * span, lat, groups)
    parts = lax.all_to_all(parts, CTX, 0, 0, tiled=True)

    order = np.zeros((owners, 8, rows, owners, owned), np.float32)
    for d in range(owners):
        for o in range(owned):
            for i in range(rows):
                order[d, 4 * o + i, i, d, o] = 1
    order = jnp.asarray(order.reshape(owners * 8, rows * heads), jnp.bfloat16)
    merged = combine(parts, order, rows, heads).reshape(owners, 8, lat // groups)

    latents = lax.all_to_all(merged, DP, 0, 0, tiled=True)
    latents = lax.all_gather(latents, CTX, axis=0, tiled=False)
    latents = latents.reshape(groups, owners * 8, lat // groups)

    select = np.zeros((near, z, rows, z, near, 8), np.float32)
    for a in range(near):
        for b in range(z):
            for i in range(rows):
                for o in range(owned):
                    select[a, b, i, b, a, 4 * o + i] = 1
    select = jnp.asarray(select.reshape(owners * rows, owners * 8), jnp.bfloat16)
    partial = project(latents, ups, select, weight)

    width = weight.shape[1]
    partial = partial.reshape(near, z * rows, width)
    partial = lax.all_to_all(partial, DP[1:], 0, 0, tiled=True)
    partial = jnp.sum(partial.astype(jnp.float32), axis=0).astype(jnp.bfloat16)
    partial = lax.all_to_all(partial.reshape(z, rows, width), DP[0], 0, 0, tiled=True)
    return jnp.sum(partial.astype(jnp.float32), axis=0).astype(jnp.bfloat16)


def solution(mesh):
    inner = Mesh(mesh.devices.reshape(8, 4, 2, 2, 2), DP + CTX)
    return jax.shard_map(
        shards,
        mesh=inner,
        in_specs=(
            P(DP, CTX, None),
            P(DP, CTX, None),
            P(DP),
            P(DP, None, None),
            P(DP, CTX),
        ),
        out_specs=P(DP, CTX),
        check_vma=False,
    )
```

time: 460 us -> 90 us (0.20)
  blocking collectives: 375 us -> 77.8 us
  waiting for transfers between devices: 34.2 us -> 0 us
  matrix products: 25.1 us -> 0 us
  starting transfers between devices: 19.6 us -> 0 us
  Pallas kernels: 0 us -> 10.4 us
    unnamed x1 -> x0, blocking collectives: 369 us -> none
    all_to_all x0 -> x4, blocking collectives: none -> 61.8 us  [the longest x1 25 us: shards(): latents = lax.all_to_all(merged, DP, 0, 0, tiled=True)]
    dot_general x10 -> x0, matrix products: 25.1 us -> none  [the longest x4 12.4 us: block_partial(): jnp.einsum('nhw,ntw->nht', query_rows, cache_rows, preferred_element_type...]
    all_to_all x1 -> x0, waiting for transfers between devices: 18.6 us -> none  [shards(): lax.all_to_all(block_rows, 'dp', split_axis=1, concat_axis=0, tiled=True)]
    ppermute x14 -> x0, waiting for transfers between devices: 15.7 us -> none  [from_behind(): return lax.ppermute(block, axis, route)]
    all_to_all x1 -> x0, starting transfers between devices: 12.5 us -> none  [shards(): lax.all_to_all(block_rows, 'dp', split_axis=1, concat_axis=0, tiled=True)]
    pallas_call x0 -> x3, Pallas kernels: none -> 10.4 us  [the longest x1 8.77 us: attend(): pl.pallas_call(functools.partial(attend_kernel, rows, heads, lat), grid=(...]
    all_gather x1 -> x2, blocking collectives: 6.15 us -> 15.9 us  [the longest x1 8.01 us: shards(): all_queries = lax.all_gather(queries, CTX, axis=1, tiled=True)]
  transfers between devices with their start and end apart: 15 -> 0, of which waited for: 7 -> 0; matrix products, arithmetic and copies ran while one was open for 6% -> 0% of each run, Pallas kernels for 0% -> 0%
where the time goes in v1:
time: 90 us; the launch traced here: 89.7 us
  blocking collectives  77.8 us (86%)
  Pallas kernels  10.4 us (12%)
  other arithmetic  1.41 us (2%)
    all_to_all x1, blocking collectives, shards(): latents = lax.all_to_all(merged, DP, 0, 0, tiled=True)  25 us
    all_to_all x1, blocking collectives, shards(): partial = lax.all_to_all(partial, DP[1:], 0, 0, tiled=True)  16.3 us
    all_to_all x1, blocking collectives, shards(): lax.all_to_all(partial.reshape(z, rows, width), DP[0], 0, 0, tiled=True)  11.3 us
    all_to_all x1, blocking collectives, shards(): parts = lax.all_to_all(parts, CTX, 0, 0, tiled=True)  9.22 us
    pallas_call x1, Pallas kernels, attend(): pl.pallas_call(functools.partial(attend_kernel, rows, heads, lat), grid=(...  8.77 us
    all_gather x1, blocking collectives, shards(): all_queries = lax.all_gather(queries, CTX, axis=1, tiled=True)  8.01 us
    all_gather x1, blocking collectives, shards(): latents = lax.all_gather(latents, CTX, axis=0, tiled=False)  7.94 us

profile of v1, /device:TPU:8, one launch (start us, length us, event | category | flops | bytes accessed | tf_op | source)
XLA Modules:
  0.0 89.7 jit_solution(2739823590741559522)
XLA Ops:
  0.0 0.0 copy-start.1
  0.0 0.0 copy-start.3
  0.0 0.0 copy-start
  0.0 0.0 copy-start.2
  0.0 8.0 %all_gather.9.query_ref = bf16[3,128,576]{2,1,0:T(8,128)(2,1)S(1)} all-gather(bf16[3,32,576]{2,1,0:T(8,128)(2,1)} %param.7), channel_id=1, replica_groups=mesh['z'=8,'x'=4,'yh'=2,'yl'=2,'core'=2] {'yl','core'}, dimensions={1}, use_global_device_ids=true | all-gather | bytes 552960 | tf_op jit(solution)/shard_map/all_gather | solution.py:151
  8.0 0.7 broadcast_subtract_fusion.length_ref
  8.7 8.8 %attend.1 = bf16[4,400,128]{2,1,0:T(8,128)(2,1)S(1)} custom-call(bf16[3,128,576]{2,1,0:T(8,128)(2,1)S(1)} %all_gather.9.query_ref, bf16[3,576,3200]{2,1,0:T(8,128)(2,1)} %bitcast.7, s32[3]{0:T(128)S(1)} %broadcast_subtract_fusion.length_ref), custom_call_target="tpu_custom_call" | custom-call | tf_op jit(solution)/shard_map/attend/pallas_call | solution.py:66
  17.5 9.2 %all_to_all.20.part_ref = bf16[4,400,128]{2,1,0:T(8,128)(2,1)S(1)} all-to-all(bf16[4,400,128]{2,1,0:T(8,128)(2,1)S(1)} %attend.1), channel_id=1, replica_groups=mesh['z'=8,'x'=4,'yh'=2,'yl'=2,'core'=2] {'yl','core'}, dimensions={0} | all-to-all | bytes 819200 | tf_op jit(solution)/shard_map/all_to_all | solution.py:153
  26.7 0.0 copy-done.1
  26.7 0.7 combine.1
  27.4 25.0 %all_to_all.21 = bf16[64,8,128]{2,1,0:T(8,128)(2,1)S(1)} all-to-all(bf16[64,8,128]{2,1,0:T(8,128)(2,1)S(1)} %bitcast.6), channel_id=1, replica_groups=mesh['z'=8,'x'=4,'yh'=2,'yl'=2,'core'=2] {'z','x','yh'}, dimensions={0} | all-to-all | bytes 262144 | tf_op jit(solution)/shard_map/all_to_all | solution.py:163
  52.4 7.9 %all-gather = bf16[256,8,128]{2,1,0:T(8,128)(2,1)S(1)} all-gather(bf16[64,8,128]{2,1,0:T(8,128)(2,1)S(1)} %all_to_all.21), channel_id=2, replica_groups=mesh['z'=8,'x'=4,'yh'=2,'yl'=2,'core'=2] {'yl','core'}, dimensions={0}, use_global_device_ids=true | all-gather | bytes 655360 | tf_op jit(solution)/shard_map/all_gather | solution.py:164
  60.3 0.0 copy-done.3
  60.3 0.0 copy-done
  60.3 0.0 copy-done.2
  60.3 0.9 %project.1 = bf16[192,1792]{1,0:T(8,128)(2,1)S(1)} custom-call(bf16[4,512,128]{2,1,0:T(8,128)(2,1)S(1)} %bitcast.5, bf16[2,512,128]{2,1,0:T(8,128)(2,1)S(1)} %copy-done.2, bf16[192,512]{1,0:T(8,128)(2,1)S(1)} %copy-done.3, bf16[256,1792]{1,0:T(8,128)(2,1)S(1)} %copy-done), custom_call_target="tpu_custom_call" | custom-call | tf_op jit(solution)/shard_map/project/pallas_call | solution.py:130
  61.3 16.3 %all_to_all.22 = bf16[8,24,1792]{2,1,0:T(8,128)(2,1)S(1)} all-to-all(bf16[8,24,1792]{2,1,0:T(8,128)(2,1)S(1)} %bitcast.4), channel_id=1, replica_groups=mesh['z'=8,'x'=4,'yh'=2,'yl'=2,'core'=2] {'x','yh'}, dimensions={0} | all-to-all | bytes 1376256 | tf_op jit(solution)/shard_map/all_to_all | solution.py:178
  77.6 0.1 reduce_sum.24
  77.7 11.3 %all_to_all.23 = bf16[8,3,1792]{2,1,0:T(4,128)(2,1)S(1)} all-to-all(bf16[8,3,1792]{2,1,0:T(4,128)(2,1)S(1)} %reshape.15), channel_id=1, replica_groups=mesh['z'=8,'x'=4,'yh'=2,'yl'=2,'core'=2] {'z'}, dimensions={0} | all-to-all | bytes 172032 | tf_op jit(solution)/shard_map/all_to_all | solution.py:180
  89.0 0.7 reduce_sum.25
  (1 shorter events, 0.0 us)
Async XLA Ops:
  0.0 26.7 %copy-start.1 = (bf16[512,384]{1,0:T(8,128)(2,1)S(1)}, bf16[512,384]{1,0:T(8,128)(2,1)}, u32[]{:S(2)}) copy-start(bf16[512,384]{1,0:T(8,128)(2,1)} %constant.18.clone.order_ref) | copy-start | bytes 1179652
  0.0 60.3 %copy-start.3 = (bf16[192,512]{1,0:T(8,128)(2,1)S(1)}, bf16[192,512]{1,0:T(8,128)(2,1)}, u32[]{:S(2)}) copy-start(bf16[192,512]{1,0:T(8,128)(2,1)} %constant.19.clone.select_ref) | copy-start | bytes 589828
  0.0 60.3 %copy-start = (bf16[256,1792]{1,0:T(8,128)(2,1)S(1)}, bf16[256,1792]{1,0:T(8,128)(2,1)}, u32[]{:S(2)}) copy-start(bf16[256,1792]{1,0:T(8,128)(2,1)} %weight_ref.1) | copy-start | bytes 2752516
  0.0 60.3 %copy-start.2 = (bf16[2,512,128]{2,1,0:T(8,128)(2,1)S(1)}, bf16[2,512,128]{2,1,0:T(8,128)(2,1)}, u32[]{:S(2)}) copy-start(bf16[2,512,128]{2,1,0:T(8,128)(2,1)} %up_ref.1) | copy-start | bytes 786436

commit v2 on v0

v2 whole, which is shorter than its diff:
```python
import functools
import math

import jax
import jax.numpy as jnp
import numpy as np
from jax import lax
from jax.experimental import pallas as pl
from jax.experimental.pallas import tpu as pltpu
from jax.sharding import Mesh, PartitionSpec as P

ROPE = 64
QK = 128
SCALE = (QK + ROPE) ** -0.5
LOG2E = math.log2(math.e)
DEAD = -1e30
DP = ("z", "x", "yh")
PEERS = ("z", "yh")
CTX = ("yl", "core")
STAT_ROWS = 16
SLOTS = 4
VMEM = pl.BlockSpec(memory_space=pltpu.VMEM)
SMEM = pl.BlockSpec(memory_space=pltpu.SMEM)
ANY = pl.BlockSpec(memory_space=pl.ANY)


def product(a, b, dim_a, dim_b):
    return lax.dot_general(
        a, b, (((dim_a,), (dim_b,)), ((), ())), preferred_element_type=jnp.float32
    )


def swap(block, axis):
    return lax.ppermute(block, axis, [(0, 1), (1, 0)])


def call(kernel, name, out_shape, in_specs, scratch=(), out_specs=None, vmem=24, work=0):
    return pl.pallas_call(
        kernel,
        in_specs=in_specs,
        out_specs=jax.tree.map(lambda _: VMEM, out_shape) if out_specs is None else out_specs,
        out_shape=out_shape,
        scratch_shapes=list(scratch),
        compiler_params=pltpu.CompilerParams(vmem_limit_bytes=vmem << 20),
        cost_estimate=pl.CostEstimate(flops=work, bytes_accessed=work, transcendentals=0),
        name=name,
    )


def pack_kernel(up_ref, weight_ref, *refs):
    out_refs, sems = refs[:-1], refs[-1]
    owned, lat, head = up_ref.shape
    width = weight_ref.shape[1]
    copies = []
    for o in range(owned):
        pairs = [(weight_ref.at[pl.ds(o * head, head), :], out_refs[o].at[:, pl.ds(0, width)])]
        for k in range(lat // head):
            pairs.append(
                (
                    up_ref.at[o, pl.ds(k * head, head), :],
                    out_refs[o].at[:, pl.ds(width + k * head, head)],
                )
            )
        for src, dst in pairs:
            copies.append(pltpu.make_async_copy(src, dst, sems.at[len(copies)]))
    for copy in copies:
        copy.start()
    for copy in copies:
        copy.wait()


def pack(ups, weight):
    owned, lat, head = ups.shape
    shape = jax.ShapeDtypeStruct((head, weight.shape[1] + lat), jnp.bfloat16)
    ups = pltpu.with_memory_space_constraint(ups, pltpu.HBM)
    weight = pltpu.with_memory_space_constraint(weight, pltpu.HBM)
    sems = pltpu.SemaphoreType.DMA((owned * (1 + lat // head),))
    return call(
        pack_kernel, "pack", [shape] * owned, [ANY] * 2, [sems], out_specs=[ANY] * owned, vmem=1
    )(ups, weight)


def load_kernel(cache_ref, query_ref, out_cache_ref, out_query_ref, sems):
    rows = cache_ref.shape[0]
    copies = [pltpu.make_async_copy(query_ref, out_query_ref, sems.at[rows])]
    for row in range(rows):
        copies.append(
            pltpu.make_async_copy(cache_ref.at[row], out_cache_ref.at[row], sems.at[row])
        )
    for copy in copies:
        copy.start()
    for copy in copies:
        copy.wait()


def load(cache, queries):
    rows = cache.shape[0]
    cache = pltpu.with_memory_space_constraint(cache, pltpu.HBM)
    queries = pltpu.with_memory_space_constraint(queries, pltpu.HBM)
    return call(
        load_kernel,
        "load",
        [pltpu.VMEM(cache.shape, cache.dtype), pltpu.VMEM(queries.shape, queries.dtype)],
        [ANY] * 2,
        [pltpu.SemaphoreType.DMA((rows + 1,))],
        out_specs=[VMEM, VMEM],
        vmem=1,
        work=12 << 20,
    )(cache, queries)


def split_logsum(logsum):
    high = logsum.astype(jnp.bfloat16).astype(jnp.float32)
    middle = (logsum - high).astype(jnp.bfloat16).astype(jnp.float32)
    return [high, middle, logsum - high - middle]


def stat_block(logsums, width):
    parts = [part for logsum in logsums for part in split_logsum(logsum)]
    parts.append(jnp.zeros((STAT_ROWS - len(parts), parts[0].shape[1]), jnp.float32))
    block = jnp.concatenate(parts, axis=0)
    return jnp.concatenate([block, jnp.zeros((STAT_ROWS, width - block.shape[1]), jnp.float32)], axis=1)


def attend_kernel(lat, place_ref, length_ref, *refs):
    query_parts, (cache_ref, mine_ref, theirs_ref, query_ref, score_ref, weight_ref) = refs[:-6], refs[-6:]
    rows, block, _ = query_parts[0].shape
    heads = block * len(query_parts)
    span = cache_ref.shape[2]
    context, core = place_ref[0], place_ref[1]
    for k, part in enumerate(query_parts):
        first = pl.multiple_of((context ^ k) * block, block)
        for row in range(rows):
            query_ref[row, pl.ds(first, block), :] = part[row]

    positions = lax.broadcasted_iota(jnp.int32, (1, span), 1) + context * span

    def score(row):
        scores = product(query_ref[row], cache_ref[row], 1, 0)
        scores = jnp.where(positions < length_ref[row], scores, DEAD)
        score_ref[row % 2] = scores
        return jnp.max(scores, axis=1, keepdims=True)

    def weigh(row, peak):
        weights = jnp.exp2((score_ref[row % 2] - peak) * (SCALE * LOG2E))
        weight_ref[row % 2] = weights.astype(jnp.bfloat16)
        return jnp.sum(weights, axis=1, keepdims=True)

    half = lat // 2
    logsums = []

    def mix(row, peak, total):
        mixed = product(weight_ref[row % 2], cache_ref[row, :lat], 1, 1)
        mixed = (mixed / total).astype(jnp.bfloat16).astype(jnp.float32)
        low, high = mixed[:, :half], mixed[:, half:]
        place = slice(row * heads, (row + 1) * heads)
        mine_ref[place, :] = jnp.where(core == 0, low, high).astype(jnp.bfloat16)
        theirs_ref[place, :] = jnp.where(core == 0, high, low).astype(jnp.bfloat16)
        logsum = peak * SCALE + jnp.log(total)
        logsums.append(jnp.broadcast_to(logsum, (heads, heads)).T[0:1])

    peak = score(0)
    for row in range(rows):
        total = weigh(row, peak)
        following = score(row + 1) if row + 1 < rows else None
        mix(row, peak, total)
        peak = following
    stats = stat_block(logsums, half).astype(jnp.bfloat16)
    mine_ref[rows * heads :, :] = stats
    theirs_ref[rows * heads :, :] = stats


def attend(places, lengths, query_parts, cache, lat):
    rows, block, width = query_parts[0].shape
    heads = block * len(query_parts)
    span = cache.shape[2]
    shape = jax.ShapeDtypeStruct((rows * heads + STAT_ROWS, lat // 2), jnp.bfloat16)
    cache = pltpu.with_memory_space_constraint(cache, pltpu.VMEM)
    return call(
        functools.partial(attend_kernel, lat),
        "attend",
        [shape, shape],
        [SMEM, SMEM] + [VMEM] * (len(query_parts) + 1),
        [
            pltpu.VMEM((rows, heads, width), jnp.bfloat16),
            pltpu.VMEM((2, heads, span), jnp.float32),
            pltpu.VMEM((2, heads, span), jnp.bfloat16),
        ],
    )(places, lengths, *query_parts, cache)


def merge_states(rows, heads, refs):
    stats = [ref[rows * heads :, :heads].astype(jnp.float32) for ref in refs]
    shares, merged_logsums = [], []
    for row in range(rows):
        logsums = [sum(s[3 * row + k : 3 * row + k + 1] for k in range(3)) for s in stats]
        peak = functools.reduce(jnp.maximum, logsums)
        factors = [jnp.exp(v - peak) for v in logsums]
        total = functools.reduce(jnp.add, factors)
        shares += [f / total for f in factors]
        merged_logsums.append(peak + jnp.log(total))
    shares.append(jnp.zeros((heads - len(shares), heads), jnp.float32))
    shares = jnp.concatenate(shares, axis=0).T
    merged = []
    for row in range(rows):
        terms = []
        for c, ref in enumerate(refs):
            column = row * len(refs) + c
            values = ref[row * heads : (row + 1) * heads, :].astype(jnp.float32)
            terms.append(shares[:, column : column + 1] * values)
        merged.append(sum(terms).astype(jnp.bfloat16))
    return merged, merged_logsums


def merge_kernel(rows, heads, a_ref, b_ref, out_ref):
    merged, logsums = merge_states(rows, heads, (a_ref, b_ref))
    for row in range(rows):
        out_ref[row * heads : (row + 1) * heads, :] = merged[row]
    out_ref[rows * heads :, :] = stat_block(logsums, out_ref.shape[1]).astype(jnp.bfloat16)


def merge(a, b, rows, heads):
    shape = jax.ShapeDtypeStruct(a.shape, jnp.bfloat16)
    return call(functools.partial(merge_kernel, rows, heads), "merge", shape, [VMEM, VMEM])(a, b)


def finish_kernel(rows, heads, owned, sizes, a_ref, b_ref, out_ref):
    merged, _ = merge_states(rows, heads, (a_ref, b_ref))
    merged = jnp.concatenate(merged, axis=0)
    _, x, yh = sizes
    place = lax.broadcasted_iota(jnp.int32, (rows * heads, 1), 0)
    row, place = place % rows, place // rows
    head, place = place % owned, place // owned
    across, place = place % x, place // x
    side, deep = place % yh, place // yh
    source = row * heads + ((deep * x + across) * yh + side) * owned + head
    columns = lax.broadcasted_iota(jnp.int32, (1, rows * heads), 1)
    order = jnp.where(columns == source, 1.0, 0.0).astype(jnp.bfloat16)
    out_ref[...] = product(order, merged, 1, 0).astype(jnp.bfloat16)


def finish(a, b, rows, heads, owned, sizes):
    shape = jax.ShapeDtypeStruct((rows * heads, a.shape[1]), jnp.bfloat16)
    kernel = functools.partial(finish_kernel, rows, heads, owned, sizes)
    return call(kernel, "finish", shape, [VMEM] * 2)(a, b)


def project_kernel(rows, owned, width, place_ref, mine_ref, theirs_ref, *refs):
    tiles, (out_ref, sorted_ref) = refs[:-2], refs[-2:]
    core, here = place_ref[1], place_ref[2]
    half = mine_ref.shape[1]
    peers = out_ref.shape[0]
    count = mine_ref.shape[0] // (peers * rows)
    target = lax.broadcasted_iota(jnp.int32, (sorted_ref.shape[0], 1), 0)
    slot, target = target % SLOTS, target // SLOTS
    holder, group = target % peers, target // peers
    source = jnp.where(slot < rows, (holder * count + group) * rows + slot, -1)
    columns = lax.broadcasted_iota(jnp.int32, (1, mine_ref.shape[0]), 1)
    select = jnp.where(columns == source, 1.0, 0.0).astype(jnp.bfloat16)
    mine = product(select, mine_ref[...], 1, 0).astype(jnp.bfloat16)
    theirs = product(select, theirs_ref[...], 1, 0).astype(jnp.bfloat16)
    sorted_ref[:, :half] = jnp.where(core == 0, mine, theirs)
    sorted_ref[:, half:] = jnp.where(core == 0, theirs, mine)
    slots = peers * SLOTS
    ring = count // owned
    result = None
    for k, distance in enumerate((0, ring - 1, 1, 2)):
        pieces = tiles[k * owned : (k + 1) * owned]
        heads_out = []
        for o, tile in enumerate(pieces):
            head = tile.shape[0]
            first = ((here + distance) % ring * owned + o) * slots
            lines = sorted_ref[pl.ds(pl.multiple_of(first, slots), slots), :]
            up = [tile[:, width + j * head : width + (j + 1) * head] for j in range(2 * half // head)]
            up = jnp.concatenate(up, axis=0)
            heads_out.append(product(lines, up, 1, 0).astype(jnp.bfloat16))
        weight = jnp.concatenate([tile[:, :width] for tile in pieces], axis=0)
        term = product(jnp.concatenate(heads_out, axis=1), weight, 1, 0)
        result = term if result is None else result + term
    result = result.astype(jnp.bfloat16)
    for d in range(peers):
        out_ref[d] = result[d * SLOTS : d * SLOTS + rows, :]


def project(places, mine, theirs, tiles, peers, rows, owned, width):
    ring = mine.shape[0] // (peers * rows * owned)
    lines = ring * owned * peers * SLOTS
    return call(
        functools.partial(project_kernel, rows, owned, width),
        "project",
        jax.ShapeDtypeStruct((peers, rows, width), jnp.bfloat16),
        [SMEM] + [VMEM] * (2 + len(tiles)),
        [pltpu.VMEM((lines, 2 * mine.shape[1]), jnp.bfloat16)],
    )(places, mine, theirs, *tiles)


def from_x(block, distance):
    size = lax.axis_size("x")
    return lax.ppermute(block, "x", [(i, (i + distance) % size) for i in range(size)])


def shards(queries, cache, lengths, ups, weight):
    rows = queries.shape[0]
    owned, lat, _ = ups.shape
    sizes = tuple(lax.axis_size(a) for a in DP)
    heads = math.prod(sizes) * owned
    peers = math.prod(lax.axis_size(a) for a in PEERS)
    places = jnp.stack([lax.axis_index(CTX), lax.axis_index("core"), lax.axis_index("x")])

    across = swap(queries, "yl")
    partner = swap(queries, "core")
    own = pack(ups, weight)
    behind, ahead = from_x(own[0], 1), from_x(own[1], -1)

    cache, held = load(jnp.swapaxes(cache, 1, 2), queries)
    query_parts = [held, partner, across, swap(across, "core")]
    mine, theirs = attend(places, lengths, query_parts, cache, lat)
    state = merge(mine, swap(theirs, "core"), rows, heads)
    state, behind, ahead, own = lax.optimization_barrier((state, behind, ahead, own))
    tiles = [
        *own,
        *(behind, from_x(own[1], 1)),
        *(from_x(own[0], -1), ahead),
        *(from_x(behind, 1), from_x(ahead, -1)),
    ]
    latents = finish(state, swap(state, "yl"), rows, heads, owned, sizes)

    latents = latents.reshape(peers, -1, lat // 2)
    latents = lax.all_to_all(latents, PEERS, 0, 0, tiled=True)
    latents = latents.reshape(rows * heads, lat // 2)
    partial = project(
        places, latents, swap(latents, "core"), tiles, peers, rows, owned, weight.shape[1]
    )
    partial = lax.all_to_all(partial, PEERS, 0, 0, tiled=True)
    return jnp.sum(partial.astype(jnp.float32), axis=0).astype(jnp.bfloat16)


def solution(mesh):
    inner = Mesh(mesh.devices.reshape(8, 4, 2, 2, 2), DP + CTX)
    return jax.shard_map(
        shards,
        mesh=inner,
        in_specs=(
            P(DP, CTX, None),
            P(DP, CTX, None),
            P(DP),
            P(DP, None, None),
            P(DP, CTX),
        ),
        out_specs=P(DP, CTX),
        check_vma=False,
    )
```

time: 460 us -> 76.1 us (0.17)
  blocking collectives: 375 us -> 41.7 us
  waiting for transfers between devices: 34.2 us -> 3.75 us
  matrix products: 25.1 us -> 0 us
  Pallas kernels: 0 us -> 15.1 us
  starting transfers between devices: 19.6 us -> 13.7 us
    unnamed x1 -> x0, blocking collectives: 369 us -> none
    all_to_all x0 -> x2, blocking collectives: none -> 41.7 us  [the longest x1 21 us: shards(): latents = lax.all_to_all(latents, PEERS, 0, 0, tiled=True)]
    dot_general x10 -> x0, matrix products: 25.1 us -> none  [the longest x4 12.4 us: block_partial(): jnp.einsum('nhw,ntw->nht', query_rows, cache_rows, preferred_element_type...]
    all_to_all x1 -> x0, waiting for transfers between devices: 18.6 us -> none  [shards(): lax.all_to_all(block_rows, 'dp', split_axis=1, concat_axis=0, tiled=True)]
    pallas_call x0 -> x6, Pallas kernels: none -> 15.1 us  [the longest x1 5.94 us: attend(): call(functools.partial(attend_kernel, lat), 'attend', [shape, shape], [SM...]
    all_to_all x1 -> x0, starting transfers between devices: 12.5 us -> none  [shards(): lax.all_to_all(block_rows, 'dp', split_axis=1, concat_axis=0, tiled=True)]
    ppermute x14 -> x12, waiting for transfers between devices: 15.7 us -> 3.75 us  [the longest x6 3.59 us: swap(): return lax.ppermute(block, axis, [(0, 1), (1, 0)])]
    ppermute x14 -> x12, starting transfers between devices: 7.18 us -> 13.7 us  [the longest x6 9.79 us: from_x(): lax.ppermute(block, 'x', [(i, (i + distance) % size) for i in range(size)])]
  transfers between devices with their start and end apart: 15 -> 12, of which waited for: 7 -> 5; matrix products, arithmetic and copies ran while one was open for 6% -> 0% of each run, Pallas kernels for 0% -> 15%
where the time goes in v2:
time: 76.1 us; the launch traced here: 75.1 us
  blocking collectives  41.7 us (55%)
  Pallas kernels  15.1 us (20%)
  starting transfers between devices  13.7 us (18%)
  waiting for transfers between devices  3.75 us (5%)
  other arithmetic  0.78 us (1%)
    all_to_all x1, blocking collectives, shards(): latents = lax.all_to_all(latents, PEERS, 0, 0, tiled=True)  21 us
    all_to_all x1, blocking collectives, shards(): partial = lax.all_to_all(partial, PEERS, 0, 0, tiled=True)  20.7 us
    ppermute x6, starting transfers between devices, from_x(): lax.ppermute(block, 'x', [(i, (i + distance) % size) for i in range(size)])  9.79 us
    pallas_call x1, Pallas kernels, attend(): call(functools.partial(attend_kernel, lat), 'attend', [shape, shape], [SM...  5.94 us
    pallas_call x1, Pallas kernels, load(): call(load_kernel, 'load', [pltpu.VMEM(cache.shape, cache.dtype), pltpu.VM...  4.31 us
    ppermute x6, starting transfers between devices, swap(): return lax.ppermute(block, axis, [(0, 1), (1, 0)])  3.88 us
    ppermute x6, waiting for transfers between devices, swap(): return lax.ppermute(block, axis, [(0, 1), (1, 0)])  3.59 us
    pallas_call x1, Pallas kernels, project(): call(functools.partial(project_kernel, rows, owned, width), 'project', ja...  2.17 us
  transfers between devices with their start and end apart: 12, of which 5 were waited for; matrix products, arithmetic and copies ran while one was open for 0% of the time, Pallas kernels for 15%

profile of v2, /device:TPU:8, one launch (start us, length us, event | category | flops | bytes accessed | tf_op | source)
XLA Modules:
  0.0 75.1 jit_solution(4325987080849076334)
XLA Ops:
  0.0 0.0 copy-start
  0.0 1.3 %pack.1 = (bf16[128,2304]{1,0:T(8,128)(2,1)S(1)}, bf16[128,2304]{1,0:T(8,128)(2,1)S(1)}) custom-call(bf16[2,512,128]{2,1,0:T(8,128)(2,1)} %up_ref.1, bf16[256,1792]{1,0:T(8,128)(2,1)} %weight_ref.1), custom_call_target="tpu_custom_call" | custom-call | tf_op jit(solution)/shard_map/pack/pallas_call | solution.py:78
  1.3 1.6 %collective-permute-start.4 = (bf16[128,2304]{1,0:T(8,128)(2,1)S(1)}, bf16[128,2304]{1,0:T(8,128)(2,1)S(1)}, u32[]{:S(2)}, u32[]{:S(2)}) collective-permute-start(bf16[128,2304]{1,0:T(8,128)(2,1)S(1)} %get-tuple-element.23.refs_0_), channel_id=1, source_target_pairs={{0,8},{8,16},{16,24},{24,0},{1,9},{9,17},{17,25},{25,1},{2,10},{10... | collective-permute-start | bytes 1769480 | tf_op jit(solution)/shard_map/ppermute | solution.py:299
  2.9 1.7 %collective-permute-start.5 = (bf16[128,2304]{1,0:T(8,128)(2,1)S(1)}, bf16[128,2304]{1,0:T(8,128)(2,1)S(1)}, u32[]{:S(2)}, u32[]{:S(2)}) collective-permute-start(bf16[128,2304]{1,0:T(8,128)(2,1)S(1)} %get-tuple-element.24.refs_1_), channel_id=1, source_target_pairs={{0,24},{8,0},{16,8},{24,16},{1,25},{9,1},{17,9},{25,17},{2,26},{10... | collective-permute-start | bytes 1769480 | tf_op jit(solution)/shard_map/ppermute | solution.py:299
  4.7 2.2 %collective-permute-start.1 = (bf16[3,32,576]{2,1,0:T(8,128)(2,1)}, bf16[3,32,576]{2,1,0:T(8,128)(2,1)S(1)}, u32[]{:S(2)}, u32[]{:S(2)}) collective-permute-start(bf16[3,32,576]{2,1,0:T(8,128)(2,1)} %query_ref.1), channel_id=1, source_target_pairs={{0,2},{2,0},{1,3},{3,1},{4,6},{6,4},{5,7},{7,5},{8,10},{10,8},{9,1... | collective-permute-start | bytes 331784 | tf_op jit(solution)/shard_map/ppermute | solution.py:34
  6.8 0.0 collective-permute-start
  6.8 4.3 %load.1 = (bf16[3,576,3200]{2,1,0:T(8,128)(2,1)S(1)}, bf16[3,32,576]{2,1,0:T(8,128)(2,1)S(1)}) custom-call(bf16[3,576,3200]{2,1,0:T(8,128)(2,1)} %bitcast.9, bf16[3,32,576]{2,1,0:T(8,128)(2,1)} %query_ref.1), custom_call_target="tpu_custom_call" | custom-call | flops 12582912 | bytes 12582912 | tf_op jit(solution)/shard_map/load/pallas_call | solution.py:100
  11.2 0.0 collective-permute-done.1.refs_2_
  11.2 0.6 collective-permute-start.2
  11.8 0.1 pad_add_fusion.place_ref
  11.8 0.0 collective-permute-done.refs_1_
  11.8 0.9 %collective-permute-done.2.refs_3_ = bf16[3,32,576]{2,1,0:T(8,128)(2,1)S(1)} collective-permute-done((bf16[3,32,576]{2,1,0:T(8,128)(2,1)S(1)}, bf16[3,32,576]{2,1,0:T(8,128)(2,1)S(1)}, u32[]{:S(2)}, u32[]{:S(2)}) %collective-permute-start.2) | collective-permute-done | bytes 110624 | tf_op jit(solution)/shard_map/ppermute | solution.py:34
  12.7 0.0 copy-done
  12.7 5.9 %attend.1 = (bf16[400,256]{1,0:T(8,128)(2,1)S(1)}, bf16[400,256]{1,0:T(8,128)(2,1)S(1)}) custom-call(s32[3]{0:T(128)S(1)} %pad_add_fusion.place_ref, s32[3]{0:T(128)S(1)} %copy-done, bf16[3,32,576]{2,1,0:T(8,128)(2,1)S(1)} %get-tuple-element.16.refs_0_, bf16[3,32,576]{2,1,0:T(8,128)(2,1)S(1)} %collective-permute-done.refs_1_, ...), custom_call_target="tpu_custom_call" | custom-call | tf_op jit(solution)/shard_map/attend/pallas_call | solution.py:179
  18.7 0.5 collective-permute-start.3
  19.1 1.1 %collective-permute-done.3.b_ref = bf16[400,256]{1,0:T(8,128)(2,1)S(1)} collective-permute-done((bf16[400,256]{1,0:T(8,128)(2,1)S(1)}, bf16[400,256]{1,0:T(8,128)(2,1)S(1)}, u32[]{:S(2)}, u32[]{:S(2)}) %collective-permute-start.3) | collective-permute-done | bytes 204832 | tf_op jit(solution)/shard_map/ppermute | solution.py:34
  20.2 0.3 merge.1.a_ref
  20.6 0.0 collective-permute-done.4.refs_2_
  20.6 0.0 collective-permute-done.5.refs_5_
  20.6 0.6 collective-permute-start.6
  21.2 0.0 collective-permute-start.10
  21.2 3.2 %collective-permute-start.11 = (bf16[128,2304]{1,0:T(8,128)(2,1)S(1)}, bf16[128,2304]{1,0:T(8,128)(2,1)S(1)}, u32[]{:S(2)}, u32[]{:S(2)}) collective-permute-start(bf16[128,2304]{1,0:T(8,128)(2,1)S(1)} %collective-permute-done.5.refs_5_), channel_id=1, source_target_pairs={{0,24},{8,0},{16,8},{24,16},{1,25},{9,1},{17,9},{25,17},{2,26},{10... | collective-permute-start | bytes 1769480 | tf_op jit(solution)/shard_map/ppermute | solution.py:299
  24.5 0.0 collective-permute-start.8
  24.5 3.2 %collective-permute-start.9 = (bf16[128,2304]{1,0:T(8,128)(2,1)S(1)}, bf16[128,2304]{1,0:T(8,128)(2,1)S(1)}, u32[]{:S(2)}, u32[]{:S(2)}) collective-permute-start(bf16[128,2304]{1,0:T(8,128)(2,1)S(1)} %get-tuple-element.23.refs_0_), channel_id=1, source_target_pairs={{0,24},{8,0},{16,8},{24,16},{1,25},{9,1},{17,9},{25,17},{2,26},{10... | collective-permute-start | bytes 1769480 | tf_op jit(solution)/shard_map/ppermute | solution.py:299
  27.7 0.3 collective-permute-done.6.b_ref
  28.0 1.0 %finish.1 = bf16[384,256]{1,0:T(8,128)(2,1)S(1)} custom-call(bf16[400,256]{1,0:T(8,128)(2,1)S(1)} %merge.1.a_ref, bf16[400,256]{1,0:T(8,128)(2,1)S(1)} %collective-permute-done.6.b_ref), custom_call_target="tpu_custom_call" | custom-call | tf_op jit(solution)/shard_map/finish/pallas_call | solution.py:245
  29.0 21.0 %all_to_all.10 = bf16[16,24,256]{2,1,0:T(8,128)(2,1)S(1)} all-to-all(bf16[16,24,256]{2,1,0:T(8,128)(2,1)S(1)} %bitcast.8), channel_id=1, replica_groups=mesh['z'=8,'x'=4,'yh'=2,'yl'=2,'core'=2] {'z','yh'}, dimensions={0} | all-to-all | bytes 393216 | tf_op jit(solution)/shard_map/all_to_all | solution.py:329
  50.0 0.0 collective-permute-start.7
  50.1 0.0 collective-permute-done.10.refs_6_
  50.1 0.0 collective-permute-done.11.refs_7_
  50.1 0.1 collective-permute-done.8.refs_3_
  50.2 0.0 collective-permute-done.9.refs_4_
  50.2 1.3 %collective-permute-done.7.theirs_ref = bf16[384,256]{1,0:T(8,128)(2,1)S(1)} collective-permute-done((bf16[384,256]{1,0:T(8,128)(2,1)S(1)}, bf16[384,256]{1,0:T(8,128)(2,1)S(1)}, u32[]{:S(2)}, u32[]{:S(2)}) %collective-permute-start.7) | collective-permute-done | bytes 196640 | tf_op jit(solution)/shard_map/ppermute | solution.py:34
  51.5 2.2 %project.1 = bf16[16,3,1792]{2,1,0:T(4,128)(2,1)S(1)} custom-call(s32[3]{0:T(128)S(1)} %pad_add_fusion.place_ref, bf16[384,256]{1,0:T(8,128)(2,1)S(1)} %bitcast.7, bf16[384,256]{1,0:T(8,128)(2,1)S(1)} %collective-permute-done.7.theirs_ref, bf16[128,2304]{1,0:T(8,128)(2,1)S(1)} %get-tuple-element.23.refs_0_, bf16[128,2304]{1,0:T(8,128)(2,1)S(1)} %get-tuple-element.24.refs_1_, ...), custom_call_target="tpu_custom_call" | custom-call | tf_op jit(solution)/shard_map/project/pallas_call | solution.py:288
  53.7 20.7 %all_to_all.11 = bf16[16,3,1792]{2,1,0:T(4,128)(2,1)S(1)} all-to-all(bf16[16,3,1792]{2,1,0:T(4,128)(2,1)S(1)} %project.1), channel_id=1, replica_groups=mesh['z'=8,'x'=4,'yh'=2,'yl'=2,'core'=2] {'z','yh'}, dimensions={0} | all-to-all | bytes 344064 | tf_op jit(solution)/shard_map/all_to_all | solution.py:334
  74.4 0.7 reduce_sum.12
Async XLA Ops:
  0.0 12.7 %copy-start = (s32[3]{0:T(128)S(1)}, s32[3]{0:T(128)}, u32[]{:S(2)}) copy-start(s32[3]{0:T(128)} %length_ref.1) | copy-start | bytes 40
  1.3 19.2 %collective-permute-start.4 = (bf16[128,2304]{1,0:T(8,128)(2,1)S(1)}, bf16[128,2304]{1,0:T(8,128)(2,1)S(1)}, u32[]{:S(2)}, u32[]{:S(2)}) collective-permute-start(bf16[128,2304]{1,0:T(8,128)(2,1)S(1)} %get-tuple-element.23.refs_0_), channel_id=1, source_target_pairs={{0,8},{8,16},{16,24},{24,0},{1,9},{9,17},{17,25},{25,1},{2,10},{10... | collective-permute-start | bytes 1769480 | tf_op jit(solution)/shard_map/ppermute | solution.py:299
  2.9 17.7 %collective-permute-start.5 = (bf16[128,2304]{1,0:T(8,128)(2,1)S(1)}, bf16[128,2304]{1,0:T(8,128)(2,1)S(1)}, u32[]{:S(2)}, u32[]{:S(2)}) collective-permute-start(bf16[128,2304]{1,0:T(8,128)(2,1)S(1)} %get-tuple-element.24.refs_1_), channel_id=1, source_target_pairs={{0,24},{8,0},{16,8},{24,16},{1,25},{9,1},{17,9},{25,17},{2,26},{10... | collective-permute-start | bytes 1769480 | tf_op jit(solution)/shard_map/ppermute | solution.py:299
  4.7 6.5 %collective-permute-start.1 = (bf16[3,32,576]{2,1,0:T(8,128)(2,1)}, bf16[3,32,576]{2,1,0:T(8,128)(2,1)S(1)}, u32[]{:S(2)}, u32[]{:S(2)}) collective-permute-start(bf16[3,32,576]{2,1,0:T(8,128)(2,1)} %query_ref.1), channel_id=1, source_target_pairs={{0,2},{2,0},{1,3},{3,1},{4,6},{6,4},{5,7},{7,5},{8,10},{10,8},{9,1... | collective-permute-start | bytes 331784 | tf_op jit(solution)/shard_map/ppermute | solution.py:34
  6.8 5.0 %collective-permute-start = (bf16[3,32,576]{2,1,0:T(8,128)(2,1)}, bf16[3,32,576]{2,1,0:T(8,128)(2,1)S(1)}, u32[]{:S(2)}, u32[]{:S(2)}) collective-permute-start(bf16[3,32,576]{2,1,0:T(8,128)(2,1)} %query_ref.1), channel_id=1, source_target_pairs={{0,1},{1,0},{2,3},{3,2},{4,5},{5,4},{6,7},{7,6},{8,9},{9,8},{10,11... | collective-permute-start | bytes 331784 | tf_op jit(solution)/shard_map/ppermute | solution.py:34
  11.2 1.6 %collective-permute-start.2 = (bf16[3,32,576]{2,1,0:T(8,128)(2,1)S(1)}, bf16[3,32,576]{2,1,0:T(8,128)(2,1)S(1)}, u32[]{:S(2)}, u32[]{:S(2)}) collective-permute-start(bf16[3,32,576]{2,1,0:T(8,128)(2,1)S(1)} %collective-permute-done.1.refs_2_), channel_id=1, source_target_pairs={{0,1},{1,0},{2,3},{3,2},{4,5},{5,4},{6,7},{7,6},{8,9},{9,8},{10,11... | collective-permute-start | bytes 331784 | tf_op jit(solution)/shard_map/ppermute | solution.py:34
  18.7 1.5 %collective-permute-start.3 = (bf16[400,256]{1,0:T(8,128)(2,1)S(1)}, bf16[400,256]{1,0:T(8,128)(2,1)S(1)}, u32[]{:S(2)}, u32[]{:S(2)}) collective-permute-start(bf16[400,256]{1,0:T(8,128)(2,1)S(1)} %get-tuple-element.19), channel_id=1, source_target_pairs={{0,1},{1,0},{2,3},{3,2},{4,5},{5,4},{6,7},{7,6},{8,9},{9,8},{10,11... | collective-permute-start | bytes 614408 | tf_op jit(solution)/shard_map/ppermute | solution.py:34
  20.6 7.4 %collective-permute-start.6 = (bf16[400,256]{1,0:T(8,128)(2,1)S(1)}, bf16[400,256]{1,0:T(8,128)(2,1)S(1)}, u32[]{:S(2)}, u32[]{:S(2)}) collective-permute-start(bf16[400,256]{1,0:T(8,128)(2,1)S(1)} %merge.1.a_ref), channel_id=1, source_target_pairs={{0,2},{2,0},{1,3},{3,1},{4,6},{6,4},{5,7},{7,5},{8,10},{10,8},{9,1... | collective-permute-start | bytes 614408 | tf_op jit(solution)/shard_map/ppermute | solution.py:34
  21.2 28.8 %collective-permute-start.10 = (bf16[128,2304]{1,0:T(8,128)(2,1)S(1)}, bf16[128,2304]{1,0:T(8,128)(2,1)S(1)}, u32[]{:S(2)}, u32[]{:S(2)}) collective-permute-start(bf16[128,2304]{1,0:T(8,128)(2,1)S(1)} %collective-permute-done.4.refs_2_), channel_id=1, source_target_pairs={{0,8},{8,16},{16,24},{24,0},{1,9},{9,17},{17,25},{25,1},{2,10},{10... | collective-permute-start | bytes 1769480 | tf_op jit(solution)/shard_map/ppermute | solution.py:299
  21.2 28.8 %collective-permute-start.11 = (bf16[128,2304]{1,0:T(8,128)(2,1)S(1)}, bf16[128,2304]{1,0:T(8,128)(2,1)S(1)}, u32[]{:S(2)}, u32[]{:S(2)}) collective-permute-start(bf16[128,2304]{1,0:T(8,128)(2,1)S(1)} %collective-permute-done.5.refs_5_), channel_id=1, source_target_pairs={{0,24},{8,0},{16,8},{24,16},{1,25},{9,1},{17,9},{25,17},{2,26},{10... | collective-permute-start | bytes 1769480 | tf_op jit(solution)/shard_map/ppermute | solution.py:299
  24.5 25.8 %collective-permute-start.8 = (bf16[128,2304]{1,0:T(8,128)(2,1)S(1)}, bf16[128,2304]{1,0:T(8,128)(2,1)S(1)}, u32[]{:S(2)}, u32[]{:S(2)}) collective-permute-start(bf16[128,2304]{1,0:T(8,128)(2,1)S(1)} %get-tuple-element.24.refs_1_), channel_id=1, source_target_pairs={{0,8},{8,16},{16,24},{24,0},{1,9},{9,17},{17,25},{25,1},{2,10},{10... | collective-permute-start | bytes 1769480 | tf_op jit(solution)/shard_map/ppermute | solution.py:299
  24.5 25.8 %collective-permute-start.9 = (bf16[128,2304]{1,0:T(8,128)(2,1)S(1)}, bf16[128,2304]{1,0:T(8,128)(2,1)S(1)}, u32[]{:S(2)}, u32[]{:S(2)}) collective-permute-start(bf16[128,2304]{1,0:T(8,128)(2,1)S(1)} %get-tuple-element.23.refs_0_), channel_id=1, source_target_pairs={{0,24},{8,0},{16,8},{24,16},{1,25},{9,1},{17,9},{25,17},{2,26},{10... | collective-permute-start | bytes 1769480 | tf_op jit(solution)/shard_map/ppermute | solution.py:299
  50.0 1.4 %collective-permute-start.7 = (bf16[384,256]{1,0:T(8,128)(2,1)S(1)}, bf16[384,256]{1,0:T(8,128)(2,1)S(1)}, u32[]{:S(2)}, u32[]{:S(2)}) collective-permute-start(bf16[384,256]{1,0:T(8,128)(2,1)S(1)} %bitcast.6), channel_id=1, source_target_pairs={{0,1},{1,0},{2,3},{3,2},{4,5},{5,4},{6,7},{7,6},{8,9},{9,8},{10,11... | collective-permute-start | bytes 589832 | tf_op jit(solution)/shard_map/ppermute | solution.py:34

commit v3 on v2

--- a/solution.py
+++ b/solution.py
@@ -228,14 +228,14 @@
     merged, _ = merge_states(rows, heads, (a_ref, b_ref))
     merged = jnp.concatenate(merged, axis=0)
     _, x, yh = sizes
-    place = lax.broadcasted_iota(jnp.int32, (rows * heads, 1), 0)
-    row, place = place % rows, place // rows
-    head, place = place % owned, place // owned
-    across, place = place % x, place // x
-    side, deep = place % yh, place // yh
-    source = row * heads + ((deep * x + across) * yh + side) * owned + head
-    columns = lax.broadcasted_iota(jnp.int32, (1, rows * heads), 1)
-    order = jnp.where(columns == source, 1.0, 0.0).astype(jnp.bfloat16)
+    column = lax.broadcasted_iota(jnp.int32, (1, rows * heads), 1)
+    row, head = column // heads, column % heads
+    own, head = head % owned, head // owned
+    side, head = head % yh, head // yh
+    across, deep = head % x, head // x
+    target = (((deep * yh + side) * x + across) * owned + own) * rows + row
+    lines = lax.broadcasted_iota(jnp.int32, (rows * heads, 1), 0)
+    order = jnp.where(lines == target, 1.0, 0.0).astype(jnp.bfloat16)
     out_ref[...] = product(order, merged, 1, 0).astype(jnp.bfloat16)
 
 
@@ -245,11 +245,22 @@
     return call(kernel, "finish", shape, [VMEM] * 2)(a, b)
 
 
-def project_kernel(rows, owned, width, place_ref, mine_ref, theirs_ref, *refs):
-    tiles, (out_ref, sorted_ref) = refs[:-2], refs[-2:]
+def project_lines(lines, pieces, width):
+    heads_out = []
+    for rows, tile in zip(lines, pieces):
+        head = tile.shape[0]
+        up = [tile[:, j : j + head] for j in range(width, tile.shape[1], head)]
+        heads_out.append(product(rows, jnp.concatenate(up, axis=0), 1, 0).astype(jnp.bfloat16))
+    weight = jnp.concatenate([tile[:, :width] for tile in pieces], axis=0)
+    return product(jnp.concatenate(heads_out, axis=1), weight, 1, 0)
+
+
+def near_kernel(rows, owned, width, place_ref, mine_ref, theirs_ref, *refs):
+    tiles, (sum_ref, far_ref, sorted_ref) = refs[:-3], refs[-3:]
     core, here = place_ref[1], place_ref[2]
     half = mine_ref.shape[1]
-    peers = out_ref.shape[0]
+    slots = sum_ref.shape[0]
+    peers = slots // SLOTS
     count = mine_ref.shape[0] // (peers * rows)
     target = lax.broadcasted_iota(jnp.int32, (sorted_ref.shape[0], 1), 0)
     slot, target = target % SLOTS, target // SLOTS
@@ -257,41 +268,58 @@
     source = jnp.where(slot < rows, (holder * count + group) * rows + slot, -1)
     columns = lax.broadcasted_iota(jnp.int32, (1, mine_ref.shape[0]), 1)
     select = jnp.where(columns == source, 1.0, 0.0).astype(jnp.bfloat16)
-    mine = product(select, mine_ref[...], 1, 0).astype(jnp.bfloat16)
-    theirs = product(select, theirs_ref[...], 1, 0).astype(jnp.bfloat16)
-    sorted_ref[:, :half] = jnp.where(core == 0, mine, theirs)
-    sorted_ref[:, half:] = jnp.where(core == 0, theirs, mine)
+    mine, theirs = mine_ref[...], theirs_ref[...]
+    low, high = jnp.where(core == 0, mine, theirs), jnp.where(core == 0, theirs, mine)
+    sorted_ref[:, :half] = product(select, low, 1, 0).astype(jnp.bfloat16)
+    sorted_ref[:, half:] = product(select, high, 1, 0).astype(jnp.bfloat16)
+    ring = count // owned
+
+    def lines(distance, o):
+        first = ((here + distance) % ring * owned + o) * slots
+        return sorted_ref[pl.ds(pl.multiple_of(first, slots), slots), :]
+
+    result = None
+    for k, distance in enumerate((0, ring - 1, 1)):
+        pieces = tiles[k * owned : (k + 1) * owned]
+        term = project_lines([lines(distance, o) for o in range(owned)], pieces, width)
+        result = term if result is None else result + term
+    sum_ref[...] = result
+    for o in range(owned):
+        far_ref[o * slots : (o + 1) * slots, :] = lines(2, o)
+
+
+def project_near(places, mine, theirs, tiles, peers, rows, owned, width):
+    count = mine.shape[0] // (peers * rows)
     slots = peers * SLOTS
-    ring = count // owned
-    result = None
-    for k, distance in enumerate((0, ring - 1, 1, 2)):
-        pieces = tiles[k * owned : (k + 1) * owned]
-        heads_out = []
-        for o, tile in enumerate(pieces):
-            head = tile.shape[0]
-            first = ((here + distance) % ring * owned + o) * slots
-            lines = sorted_ref[pl.ds(pl.multiple_of(first, slots), slots), :]
-            up = [tile[:, width + j * head : width + (j + 1) * head] for j in range(2 * half // head)]
-            up = jnp.concatenate(up, axis=0)
-            heads_out.append(product(lines, up, 1, 0).astype(jnp.bfloat16))
-        weight = jnp.concatenate([tile[:, :width] for tile in pieces], axis=0)
-        term = product(jnp.concatenate(heads_out, axis=1), weight, 1, 0)
-        result = term if result is None else result + term
-    result = result.astype(jnp.bfloat16)
-    for d in range(peers):
+    lat = 2 * mine.shape[1]
+    return call(
+        functools.partial(near_kernel, rows, owned, width),
+        "project_near",
+        [
+            jax.ShapeDtypeStruct((slots, width), jnp.float32),
+            jax.ShapeDtypeStruct((owned * slots, lat), jnp.bfloat16),
+        ],
+        [SMEM] + [VMEM] * (2 + len(tiles)),
+        [pltpu.VMEM((count * slots, lat), jnp.bfloat16)],
+    )(places, mine, theirs, *tiles)
+
+
+def far_kernel(rows, width, sum_ref, line_ref, *refs):
+    tiles, out_ref = refs[:-1], refs[-1]
+    slots = sum_ref.shape[0]
+    lines = [line_ref[o * slots : (o + 1) * slots, :] for o in range(len(tiles))]
+    result = (sum_ref[...] + project_lines(lines, tiles, width)).astype(jnp.bfloat16)
+    for d in range(out_ref.shape[0]):
         out_ref[d] = result[d * SLOTS : d * SLOTS + rows, :]
 
 
-def project(places, mine, theirs, tiles, peers, rows, owned, width):
-    ring = mine.shape[0] // (peers * rows * owned)
-    lines = ring * owned * peers * SLOTS
-    return call(
-        functools.partial(project_kernel, rows, owned, width),
-        "project",
+def project_far(near, lines, tiles, peers, rows, width):
+    return call(
+        functools.partial(far_kernel, rows, width),
+        "project_far",
         jax.ShapeDtypeStruct((peers, rows, width), jnp.bfloat16),
-        [SMEM] + [VMEM] * (2 + len(tiles)),
-        [pltpu.VMEM((lines, 2 * mine.shape[1]), jnp.bfloat16)],
-    )(places, mine, theirs, *tiles)
+        [VMEM] * (2 + len(tiles)),
+    )(near, lines, *tiles)
 
 
 def from_x(block, distance):
@@ -315,22 +343,20 @@
     cache, held = load(jnp.swapaxes(cache, 1, 2), queries)
     query_parts = [held, partner, across, swap(across, "core")]
     mine, theirs = attend(places, lengths, query_parts, cache, lat)
+    theirs, own = lax.optimization_barrier((theirs, own))
+    behind_too, ahead_too = from_x(own[1], 1), from_x(own[0], -1)
     state = merge(mine, swap(theirs, "core"), rows, heads)
-    state, behind, ahead, own = lax.optimization_barrier((state, behind, ahead, own))
-    tiles = [
-        *own,
-        *(behind, from_x(own[1], 1)),
-        *(from_x(own[0], -1), ahead),
-        *(from_x(behind, 1), from_x(ahead, -1)),
-    ]
+    state, behind, ahead = lax.optimization_barrier((state, behind, ahead))
+    tiles = [*own, behind, behind_too, ahead_too, ahead, from_x(behind, 1), from_x(ahead, -1)]
     latents = finish(state, swap(state, "yl"), rows, heads, owned, sizes)
 
     latents = latents.reshape(peers, -1, lat // 2)
     latents = lax.all_to_all(latents, PEERS, 0, 0, tiled=True)
     latents = latents.reshape(rows * heads, lat // 2)
-    partial = project(
-        places, latents, swap(latents, "core"), tiles, peers, rows, owned, weight.shape[1]
-    )
+    width = weight.shape[1]
+    theirs = swap(latents, "core")
+    near, lines = project_near(places, latents, theirs, tiles[:-2], peers, rows, owned, width)
+    partial = project_far(near, lines, tiles[-2:], peers, rows, width)
     partial = lax.all_to_all(partial, PEERS, 0, 0, tiled=True)
     return jnp.sum(partial.astype(jnp.float32), axis=0).astype(jnp.bfloat16)
 

time: 76.1 us -> 74.4 us (0.978)
  blocking collectives: 41.7 us -> 40.2 us
    all_to_all x1, blocking collectives: 20.7 us -> 19.2 us  [shards(): partial = lax.all_to_all(partial, PEERS, 0, 0, tiled=True)]
    pallas_call x1 -> x2, Pallas kernels: 2.17 us -> 2.36 us  [the longest x1 1.91 us: project_near(): call(functools.partial(near_kernel, rows, owned, width), 'project_near',...]
  transfers between devices with their start and end apart: 12 -> 12, of which waited for: 5 -> 4; matrix products, arithmetic and copies ran while one was open for 0% -> 0% of each run, Pallas kernels for 15% -> 18%
where the time goes in v3:
time: 74.4 us; the launch traced here: 73.4 us
  blocking collectives  40.2 us (54%)
  Pallas kernels  14.8 us (20%)
  starting transfers between devices  13.7 us (18%)
  waiting for transfers between devices  3.76 us (5%)
  other arithmetic  0.78 us (1%)
    all_to_all x1, blocking collectives, shards(): latents = lax.all_to_all(latents, PEERS, 0, 0, tiled=True)  21.1 us
    all_to_all x1, blocking collectives, shards(): partial = lax.all_to_all(partial, PEERS, 0, 0, tiled=True)  19.2 us
    ppermute x6, starting transfers between devices, from_x(): lax.ppermute(block, 'x', [(i, (i + distance) % size) for i in range(size)])  9.79 us
    pallas_call x1, Pallas kernels, attend(): call(functools.partial(attend_kernel, lat), 'attend', [shape, shape], [SM...  5.94 us
    pallas_call x1, Pallas kernels, load(): call(load_kernel, 'load', [pltpu.VMEM(cache.shape, cache.dtype), pltpu.VM...  4.31 us
    ppermute x6, starting transfers between devices, swap(): return lax.ppermute(block, axis, [(0, 1), (1, 0)])  3.88 us
    ppermute x6, waiting for transfers between devices, swap(): return lax.ppermute(block, axis, [(0, 1), (1, 0)])  3.74 us
    pallas_call x1, Pallas kernels, project_near(): call(functools.partial(near_kernel, rows, owned, width), 'project_near',...  1.91 us
  transfers between devices with their start and end apart: 12, of which 4 were waited for; matrix products, arithmetic and copies ran while one was open for 0% of the time, Pallas kernels for 18%

profile of v3, /device:TPU:8, one launch (start us, length us, event | category | flops | bytes accessed | tf_op | source)
XLA Modules:
  0.0 73.4 jit_solution(9813774476022543719)
XLA Ops:
  0.0 0.0 copy-start
  0.0 1.3 %pack.1 = (bf16[128,2304]{1,0:T(8,128)(2,1)S(1)}, bf16[128,2304]{1,0:T(8,128)(2,1)S(1)}) custom-call(bf16[2,512,128]{2,1,0:T(8,128)(2,1)} %up_ref.1, bf16[256,1792]{1,0:T(8,128)(2,1)} %weight_ref.1), custom_call_target="tpu_custom_call" | custom-call | tf_op jit(solution)/shard_map/pack/pallas_call | solution.py:78
  1.3 1.6 %collective-permute-start.4 = (bf16[128,2304]{1,0:T(8,128)(2,1)S(1)}, bf16[128,2304]{1,0:T(8,128)(2,1)S(1)}, u32[]{:S(2)}, u32[]{:S(2)}) collective-permute-start(bf16[128,2304]{1,0:T(8,128)(2,1)S(1)} %get-tuple-element.27.refs_0_), channel_id=1, source_target_pairs={{0,8},{8,16},{16,24},{24,0},{1,9},{9,17},{17,25},{25,1},{2,10},{10... | collective-permute-start | bytes 1769480 | tf_op jit(solution)/shard_map/ppermute | solution.py:327
  2.9 1.7 %collective-permute-start.5 = (bf16[128,2304]{1,0:T(8,128)(2,1)S(1)}, bf16[128,2304]{1,0:T(8,128)(2,1)S(1)}, u32[]{:S(2)}, u32[]{:S(2)}) collective-permute-start(bf16[128,2304]{1,0:T(8,128)(2,1)S(1)} %get-tuple-element.28.refs_1_), channel_id=1, source_target_pairs={{0,24},{8,0},{16,8},{24,16},{1,25},{9,1},{17,9},{25,17},{2,26},{10... | collective-permute-start | bytes 1769480 | tf_op jit(solution)/shard_map/ppermute | solution.py:327
  4.7 2.2 %collective-permute-start.1 = (bf16[3,32,576]{2,1,0:T(8,128)(2,1)}, bf16[3,32,576]{2,1,0:T(8,128)(2,1)S(1)}, u32[]{:S(2)}, u32[]{:S(2)}) collective-permute-start(bf16[3,32,576]{2,1,0:T(8,128)(2,1)} %query_ref.1), channel_id=1, source_target_pairs={{0,2},{2,0},{1,3},{3,1},{4,6},{6,4},{5,7},{7,5},{8,10},{10,8},{9,1... | collective-permute-start | bytes 331784 | tf_op jit(solution)/shard_map/ppermute | solution.py:34
  6.8 0.0 collective-permute-start
  6.8 4.3 %load.1 = (bf16[3,576,3200]{2,1,0:T(8,128)(2,1)S(1)}, bf16[3,32,576]{2,1,0:T(8,128)(2,1)S(1)}) custom-call(bf16[3,576,3200]{2,1,0:T(8,128)(2,1)} %bitcast.9, bf16[3,32,576]{2,1,0:T(8,128)(2,1)} %query_ref.1), custom_call_target="tpu_custom_call" | custom-call | flops 12582912 | bytes 12582912 | tf_op jit(solution)/shard_map/load/pallas_call | solution.py:100
  11.2 0.0 collective-permute-done.1.refs_2_
  11.2 0.6 collective-permute-start.2
  11.8 0.1 pad_add_fusion.place_ref
  11.8 0.0 collective-permute-done.refs_1_
  11.8 0.9 %collective-permute-done.2.refs_3_ = bf16[3,32,576]{2,1,0:T(8,128)(2,1)S(1)} collective-permute-done((bf16[3,32,576]{2,1,0:T(8,128)(2,1)S(1)}, bf16[3,32,576]{2,1,0:T(8,128)(2,1)S(1)}, u32[]{:S(2)}, u32[]{:S(2)}) %collective-permute-start.2) | collective-permute-done | bytes 110624 | tf_op jit(solution)/shard_map/ppermute | solution.py:34
  12.7 0.0 copy-done
  12.7 5.9 %attend.1 = (bf16[400,256]{1,0:T(8,128)(2,1)S(1)}, bf16[400,256]{1,0:T(8,128)(2,1)S(1)}) custom-call(s32[3]{0:T(128)S(1)} %pad_add_fusion.place_ref, s32[3]{0:T(128)S(1)} %copy-done, bf16[3,32,576]{2,1,0:T(8,128)(2,1)S(1)} %get-tuple-element.19.refs_0_, bf16[3,32,576]{2,1,0:T(8,128)(2,1)S(1)} %collective-permute-done.refs_1_, ...), custom_call_target="tpu_custom_call" | custom-call | tf_op jit(solution)/shard_map/attend/pallas_call | solution.py:179
  18.7 0.5 collective-permute-start.3
  19.1 1.1 %collective-permute-done.3.b_ref = bf16[400,256]{1,0:T(8,128)(2,1)S(1)} collective-permute-done((bf16[400,256]{1,0:T(8,128)(2,1)S(1)}, bf16[400,256]{1,0:T(8,128)(2,1)S(1)}, u32[]{:S(2)}, u32[]{:S(2)}) %collective-permute-start.3) | collective-permute-done | bytes 204832 | tf_op jit(solution)/shard_map/ppermute | solution.py:34
  20.2 0.3 merge.1.a_ref
  20.6 0.0 collective-permute-done.4.refs_2_
  20.6 0.0 collective-permute-done.5.refs_5_
  20.6 0.6 collective-permute-start.6
  21.2 0.0 collective-permute-start.8
  21.2 3.2 %collective-permute-start.9 = (bf16[128,2304]{1,0:T(8,128)(2,1)S(1)}, bf16[128,2304]{1,0:T(8,128)(2,1)S(1)}, u32[]{:S(2)}, u32[]{:S(2)}) collective-permute-start(bf16[128,2304]{1,0:T(8,128)(2,1)S(1)} %get-tuple-element.27.refs_0_), channel_id=1, source_target_pairs={{0,24},{8,0},{16,8},{24,16},{1,25},{9,1},{17,9},{25,17},{2,26},{10... | collective-permute-start | bytes 1769480 | tf_op jit(solution)/shard_map/ppermute | solution.py:327
  24.5 0.0 collective-permute-start.10
  24.5 3.2 %collective-permute-start.11 = (bf16[128,2304]{1,0:T(8,128)(2,1)S(1)}, bf16[128,2304]{1,0:T(8,128)(2,1)S(1)}, u32[]{:S(2)}, u32[]{:S(2)}) collective-permute-start(bf16[128,2304]{1,0:T(8,128)(2,1)S(1)} %collective-permute-done.5.refs_5_), channel_id=1, source_target_pairs={{0,24},{8,0},{16,8},{24,16},{1,25},{9,1},{17,9},{25,17},{2,26},{10... | collective-permute-start | bytes 1769480 | tf_op jit(solution)/shard_map/ppermute | solution.py:327
  27.7 0.3 collective-permute-done.6.b_ref
  28.0 0.6 finish.1
  28.6 21.1 %all_to_all.10 = bf16[16,24,256]{2,1,0:T(8,128)(2,1)S(1)} all-to-all(bf16[16,24,256]{2,1,0:T(8,128)(2,1)S(1)} %bitcast.8), channel_id=1, replica_groups=mesh['z'=8,'x'=4,'yh'=2,'yl'=2,'core'=2] {'z','yh'}, dimensions={0} | all-to-all | bytes 393216 | tf_op jit(solution)/shard_map/all_to_all | solution.py:354
  49.7 0.0 collective-permute-start.7
  49.7 0.0 collective-permute-done.8.refs_3_
  49.7 0.0 collective-permute-done.9.refs_4_
  49.7 1.4 %collective-permute-done.7.theirs_ref = bf16[384,256]{1,0:T(8,128)(2,1)S(1)} collective-permute-done((bf16[384,256]{1,0:T(8,128)(2,1)S(1)}, bf16[384,256]{1,0:T(8,128)(2,1)S(1)}, u32[]{:S(2)}, u32[]{:S(2)}) %collective-permute-start.7) | collective-permute-done | bytes 196640 | tf_op jit(solution)/shard_map/ppermute | solution.py:34
  51.1 1.9 %project_near.1 = (f32[64,1792]{1,0:T(8,128)S(1)}, bf16[128,512]{1,0:T(8,128)(2,1)S(1)}) custom-call(s32[3]{0:T(128)S(1)} %pad_add_fusion.place_ref, bf16[384,256]{1,0:T(8,128)(2,1)S(1)} %bitcast.7, bf16[384,256]{1,0:T(8,128)(2,1)S(1)} %collective-permute-done.7.theirs_ref, bf16[128,2304]{1,0:T(8,128)(2,1)S(1)} %get-tuple-element.27.refs_0_, ...), custom_call_target="tpu_custom_call" | custom-call | tf_op jit(solution)/shard_map/project_near/pallas_call | solution.py:295
  53.0 0.0 collective-permute-done.10.refs_0_
  53.0 0.0 collective-permute-done.11.refs_1_
  53.0 0.4 project_far.1
  53.5 19.2 %all_to_all.11 = bf16[16,3,1792]{2,1,0:T(4,128)(2,1)S(1)} all-to-all(bf16[16,3,1792]{2,1,0:T(4,128)(2,1)S(1)} %project_far.1), channel_id=1, replica_groups=mesh['z'=8,'x'=4,'yh'=2,'yl'=2,'core'=2] {'z','yh'}, dimensions={0} | all-to-all | bytes 344064 | tf_op jit(solution)/shard_map/all_to_all | solution.py:360
  72.6 0.7 reduce_sum.12
Async XLA Ops:
  0.0 12.7 %copy-start = (s32[3]{0:T(128)S(1)}, s32[3]{0:T(128)}, u32[]{:S(2)}) copy-start(s32[3]{0:T(128)} %length_ref.1) | copy-start | bytes 40
  1.3 19.2 %collective-permute-start.4 = (bf16[128,2304]{1,0:T(8,128)(2,1)S(1)}, bf16[128,2304]{1,0:T(8,128)(2,1)S(1)}, u32[]{:S(2)}, u32[]{:S(2)}) collective-permute-start(bf16[128,2304]{1,0:T(8,128)(2,1)S(1)} %get-tuple-element.27.refs_0_), channel_id=1, source_target_pairs={{0,8},{8,16},{16,24},{24,0},{1,9},{9,17},{17,25},{25,1},{2,10},{10... | collective-permute-start | bytes 1769480 | tf_op jit(solution)/shard_map/ppermute | solution.py:327
  2.9 17.7 %collective-permute-start.5 = (bf16[128,2304]{1,0:T(8,128)(2,1)S(1)}, bf16[128,2304]{1,0:T(8,128)(2,1)S(1)}, u32[]{:S(2)}, u32[]{:S(2)}) collective-permute-start(bf16[128,2304]{1,0:T(8,128)(2,1)S(1)} %get-tuple-element.28.refs_1_), channel_id=1, source_target_pairs={{0,24},{8,0},{16,8},{24,16},{1,25},{9,1},{17,9},{25,17},{2,26},{10... | collective-permute-start | bytes 1769480 | tf_op jit(solution)/shard_map/ppermute | solution.py:327
  4.7 6.5 %collective-permute-start.1 = (bf16[3,32,576]{2,1,0:T(8,128)(2,1)}, bf16[3,32,576]{2,1,0:T(8,128)(2,1)S(1)}, u32[]{:S(2)}, u32[]{:S(2)}) collective-permute-start(bf16[3,32,576]{2,1,0:T(8,128)(2,1)} %query_ref.1), channel_id=1, source_target_pairs={{0,2},{2,0},{1,3},{3,1},{4,6},{6,4},{5,7},{7,5},{8,10},{10,8},{9,1... | collective-permute-start | bytes 331784 | tf_op jit(solution)/shard_map/ppermute | solution.py:34
  6.8 5.0 %collective-permute-start = (bf16[3,32,576]{2,1,0:T(8,128)(2,1)}, bf16[3,32,576]{2,1,0:T(8,128)(2,1)S(1)}, u32[]{:S(2)}, u32[]{:S(2)}) collective-permute-start(bf16[3,32,576]{2,1,0:T(8,128)(2,1)} %query_ref.1), channel_id=1, source_target_pairs={{0,1},{1,0},{2,3},{3,2},{4,5},{5,4},{6,7},{7,6},{8,9},{9,8},{10,11... | collective-permute-start | bytes 331784 | tf_op jit(solution)/shard_map/ppermute | solution.py:34
  11.2 1.6 %collective-permute-start.2 = (bf16[3,32,576]{2,1,0:T(8,128)(2,1)S(1)}, bf16[3,32,576]{2,1,0:T(8,128)(2,1)S(1)}, u32[]{:S(2)}, u32[]{:S(2)}) collective-permute-start(bf16[3,32,576]{2,1,0:T(8,128)(2,1)S(1)} %collective-permute-done.1.refs_2_), channel_id=1, source_target_pairs={{0,1},{1,0},{2,3},{3,2},{4,5},{5,4},{6,7},{7,6},{8,9},{9,8},{10,11... | collective-permute-start | bytes 331784 | tf_op jit(solution)/shard_map/ppermute | solution.py:34
  18.7 1.5 %collective-permute-start.3 = (bf16[400,256]{1,0:T(8,128)(2,1)S(1)}, bf16[400,256]{1,0:T(8,128)(2,1)S(1)}, u32[]{:S(2)}, u32[]{:S(2)}) collective-permute-start(bf16[400,256]{1,0:T(8,128)(2,1)S(1)} %get-tuple-element.25), channel_id=1, source_target_pairs={{0,1},{1,0},{2,3},{3,2},{4,5},{5,4},{6,7},{7,6},{8,9},{9,8},{10,11... | collective-permute-start | bytes 614408 | tf_op jit(solution)/shard_map/ppermute | solution.py:34
  20.6 7.4 %collective-permute-start.6 = (bf16[400,256]{1,0:T(8,128)(2,1)S(1)}, bf16[400,256]{1,0:T(8,128)(2,1)S(1)}, u32[]{:S(2)}, u32[]{:S(2)}) collective-permute-start(bf16[400,256]{1,0:T(8,128)(2,1)S(1)} %merge.1.a_ref), channel_id=1, source_target_pairs={{0,2},{2,0},{1,3},{3,1},{4,6},{6,4},{5,7},{7,5},{8,10},{10,8},{9,1... | collective-permute-start | bytes 614408 | tf_op jit(solution)/shard_map/ppermute | solution.py:34
  21.2 28.4 %collective-permute-start.8 = (bf16[128,2304]{1,0:T(8,128)(2,1)S(1)}, bf16[128,2304]{1,0:T(8,128)(2,1)S(1)}, u32[]{:S(2)}, u32[]{:S(2)}) collective-permute-start(bf16[128,2304]{1,0:T(8,128)(2,1)S(1)} %get-tuple-element.28.refs_1_), channel_id=1, source_target_pairs={{0,8},{8,16},{16,24},{24,0},{1,9},{9,17},{17,25},{25,1},{2,10},{10... | collective-permute-start | bytes 1769480 | tf_op jit(solution)/shard_map/ppermute | solution.py:327
  21.2 28.4 %collective-permute-start.9 = (bf16[128,2304]{1,0:T(8,128)(2,1)S(1)}, bf16[128,2304]{1,0:T(8,128)(2,1)S(1)}, u32[]{:S(2)}, u32[]{:S(2)}) collective-permute-start(bf16[128,2304]{1,0:T(8,128)(2,1)S(1)} %get-tuple-element.27.refs_0_), channel_id=1, source_target_pairs={{0,24},{8,0},{16,8},{24,16},{1,25},{9,1},{17,9},{25,17},{2,26},{10... | collective-permute-start | bytes 1769480 | tf_op jit(solution)/shard_map/ppermute | solution.py:327
  24.5 28.6 %collective-permute-start.10 = (bf16[128,2304]{1,0:T(8,128)(2,1)S(1)}, bf16[128,2304]{1,0:T(8,128)(2,1)S(1)}, u32[]{:S(2)}, u32[]{:S(2)}) collective-permute-start(bf16[128,2304]{1,0:T(8,128)(2,1)S(1)} %collective-permute-done.4.refs_2_), channel_id=1, source_target_pairs={{0,8},{8,16},{16,24},{24,0},{1,9},{9,17},{17,25},{25,1},{2,10},{10... | collective-permute-start | bytes 1769480 | tf_op jit(solution)/shard_map/ppermute | solution.py:327
  24.5 28.6 %collective-permute-start.11 = (bf16[128,2304]{1,0:T(8,128)(2,1)S(1)}, bf16[128,2304]{1,0:T(8,128)(2,1)S(1)}, u32[]{:S(2)}, u32[]{:S(2)}) collective-permute-start(bf16[128,2304]{1,0:T(8,128)(2,1)S(1)} %collective-permute-done.5.refs_5_), channel_id=1, source_target_pairs={{0,24},{8,0},{16,8},{24,16},{1,25},{9,1},{17,9},{25,17},{2,26},{10... | collective-permute-start | bytes 1769480 | tf_op jit(solution)/shard_map/ppermute | solution.py:327
  49.7 1.4 %collective-permute-start.7 = (bf16[384,256]{1,0:T(8,128)(2,1)S(1)}, bf16[384,256]{1,0:T(8,128)(2,1)S(1)}, u32[]{:S(2)}, u32[]{:S(2)}) collective-permute-start(bf16[384,256]{1,0:T(8,128)(2,1)S(1)} %bitcast.6), channel_id=1, source_target_pairs={{0,1},{1,0},{2,3},{3,2},{4,5},{5,4},{6,7},{7,6},{8,9},{9,8},{10,11... | collective-permute-start | bytes 589832 | tf_op jit(solution)/shard_map/ppermute | solution.py:34

commit v4 on v3

--- a/solution.py
+++ b/solution.py
@@ -322,6 +322,18 @@
     )(near, lines, *tiles)
 
 
+def total_kernel(part_ref, out_ref):
+    parts = [part_ref[k].astype(jnp.float32) for k in range(part_ref.shape[0])]
+    while len(parts) > 1:
+        parts = [a + b for a, b in zip(parts[::2], parts[1::2])]
+    out_ref[...] = parts[0].astype(jnp.bfloat16)
+
+
+def total(parts):
+    shape = jax.ShapeDtypeStruct(parts.shape[1:], jnp.bfloat16)
+    return call(total_kernel, "total", shape, [VMEM])(parts)
+
+
 def from_x(block, distance):
     size = lax.axis_size("x")
     return lax.ppermute(block, "x", [(i, (i + distance) % size) for i in range(size)])
@@ -343,7 +355,6 @@
     cache, held = load(jnp.swapaxes(cache, 1, 2), queries)
     query_parts = [held, partner, across, swap(across, "core")]
     mine, theirs = attend(places, lengths, query_parts, cache, lat)
-    theirs, own = lax.optimization_barrier((theirs, own))
     behind_too, ahead_too = from_x(own[1], 1), from_x(own[0], -1)
     state = merge(mine, swap(theirs, "core"), rows, heads)
     state, behind, ahead = lax.optimization_barrier((state, behind, ahead))
@@ -358,7 +369,7 @@
     near, lines = project_near(places, latents, theirs, tiles[:-2], peers, rows, owned, width)
     partial = project_far(near, lines, tiles[-2:], peers, rows, width)
     partial = lax.all_to_all(partial, PEERS, 0, 0, tiled=True)
-    return jnp.sum(partial.astype(jnp.float32), axis=0).astype(jnp.bfloat16)
+    return total(partial)
 
 
 def solution(mesh):

time: 74.4 us -> 74.3 us (level)
  no operation moved by 1% of the time
where the time goes in v4:
time: 74.3 us; the launch traced here: 73.3 us
  blocking collectives  40.2 us (54%)
  Pallas kernels  15.5 us (21%)
  starting transfers between devices  13.7 us (18%)
  waiting for transfers between devices  3.76 us (5%)
    all_to_all x1, blocking collectives, shards(): latents = lax.all_to_all(latents, PEERS, 0, 0, tiled=True)  21.1 us
    all_to_all x1, blocking collectives, shards(): partial = lax.all_to_all(partial, PEERS, 0, 0, tiled=True)  19.2 us
    ppermute x6, starting transfers between devices, from_x(): lax.ppermute(block, 'x', [(i, (i + distance) % size) for i in range(size)])  9.79 us
    pallas_call x1, Pallas kernels, attend(): call(functools.partial(attend_kernel, lat), 'attend', [shape, shape], [SM...  5.94 us
    pallas_call x1, Pallas kernels, load(): call(load_kernel, 'load', [pltpu.VMEM(cache.shape, cache.dtype), pltpu.VM...  4.31 us
    ppermute x6, starting transfers between devices, swap(): return lax.ppermute(block, axis, [(0, 1), (1, 0)])  3.88 us
    ppermute x6, waiting for transfers between devices, swap(): return lax.ppermute(block, axis, [(0, 1), (1, 0)])  3.74 us
    pallas_call x1, Pallas kernels, project_near(): call(functools.partial(near_kernel, rows, owned, width), 'project_near',...  1.91 us
  transfers between devices with their start and end apart: 12, of which 4 were waited for; matrix products, arithmetic and copies ran while one was open for 0% of the time, Pallas kernels for 18%

profile of v4, /device:TPU:8, one launch (start us, length us, event | category | flops | bytes accessed | tf_op | source)
XLA Modules:
  0.0 73.3 jit_solution(17192987977893182902)
XLA Ops:
  0.0 0.0 copy-start
  0.0 1.3 %pack.1 = (bf16[128,2304]{1,0:T(8,128)(2,1)S(1)}, bf16[128,2304]{1,0:T(8,128)(2,1)S(1)}) custom-call(bf16[2,512,128]{2,1,0:T(8,128)(2,1)} %up_ref.1, bf16[256,1792]{1,0:T(8,128)(2,1)} %weight_ref.1), custom_call_target="tpu_custom_call" | custom-call | tf_op jit(solution)/shard_map/pack/pallas_call | solution.py:78
  1.3 1.6 %collective-permute-start.4 = (bf16[128,2304]{1,0:T(8,128)(2,1)S(1)}, bf16[128,2304]{1,0:T(8,128)(2,1)S(1)}, u32[]{:S(2)}, u32[]{:S(2)}) collective-permute-start(bf16[128,2304]{1,0:T(8,128)(2,1)S(1)} %get-tuple-element.20.refs_0_), channel_id=1, source_target_pairs={{0,8},{8,16},{16,24},{24,0},{1,9},{9,17},{17,25},{25,1},{2,10},{10... | collective-permute-start | bytes 1769480 | tf_op jit(solution)/shard_map/ppermute | solution.py:339
  2.9 1.7 %collective-permute-start.5 = (bf16[128,2304]{1,0:T(8,128)(2,1)S(1)}, bf16[128,2304]{1,0:T(8,128)(2,1)S(1)}, u32[]{:S(2)}, u32[]{:S(2)}) collective-permute-start(bf16[128,2304]{1,0:T(8,128)(2,1)S(1)} %get-tuple-element.21.refs_1_), channel_id=1, source_target_pairs={{0,24},{8,0},{16,8},{24,16},{1,25},{9,1},{17,9},{25,17},{2,26},{10... | collective-permute-start | bytes 1769480 | tf_op jit(solution)/shard_map/ppermute | solution.py:339
  4.7 2.2 %collective-permute-start.1 = (bf16[3,32,576]{2,1,0:T(8,128)(2,1)}, bf16[3,32,576]{2,1,0:T(8,128)(2,1)S(1)}, u32[]{:S(2)}, u32[]{:S(2)}) collective-permute-start(bf16[3,32,576]{2,1,0:T(8,128)(2,1)} %query_ref.1), channel_id=1, source_target_pairs={{0,2},{2,0},{1,3},{3,1},{4,6},{6,4},{5,7},{7,5},{8,10},{10,8},{9,1... | collective-permute-start | bytes 331784 | tf_op jit(solution)/shard_map/ppermute | solution.py:34
  6.8 0.0 collective-permute-start
  6.8 4.3 %load.1 = (bf16[3,576,3200]{2,1,0:T(8,128)(2,1)S(1)}, bf16[3,32,576]{2,1,0:T(8,128)(2,1)S(1)}) custom-call(bf16[3,576,3200]{2,1,0:T(8,128)(2,1)} %bitcast.9, bf16[3,32,576]{2,1,0:T(8,128)(2,1)} %query_ref.1), custom_call_target="tpu_custom_call" | custom-call | flops 12582912 | bytes 12582912 | tf_op jit(solution)/shard_map/load/pallas_call | solution.py:100
  11.2 0.0 collective-permute-done.1.refs_2_
  11.2 0.6 collective-permute-start.2
  11.8 0.1 pad_add_fusion.place_ref
  11.8 0.0 collective-permute-done.refs_1_
  11.8 0.9 %collective-permute-done.2.refs_3_ = bf16[3,32,576]{2,1,0:T(8,128)(2,1)S(1)} collective-permute-done((bf16[3,32,576]{2,1,0:T(8,128)(2,1)S(1)}, bf16[3,32,576]{2,1,0:T(8,128)(2,1)S(1)}, u32[]{:S(2)}, u32[]{:S(2)}) %collective-permute-start.2) | collective-permute-done | bytes 110624 | tf_op jit(solution)/shard_map/ppermute | solution.py:34
  12.7 0.0 copy-done
  12.7 5.9 %attend.1 = (bf16[400,256]{1,0:T(8,128)(2,1)S(1)}, bf16[400,256]{1,0:T(8,128)(2,1)S(1)}) custom-call(s32[3]{0:T(128)S(1)} %pad_add_fusion.place_ref, s32[3]{0:T(128)S(1)} %copy-done, bf16[3,32,576]{2,1,0:T(8,128)(2,1)S(1)} %get-tuple-element.16.refs_0_, bf16[3,32,576]{2,1,0:T(8,128)(2,1)S(1)} %collective-permute-done.refs_1_, ...), custom_call_target="tpu_custom_call" | custom-call | tf_op jit(solution)/shard_map/attend/pallas_call | solution.py:179
  18.7 0.5 collective-permute-start.3
  19.1 1.1 %collective-permute-done.3.b_ref = bf16[400,256]{1,0:T(8,128)(2,1)S(1)} collective-permute-done((bf16[400,256]{1,0:T(8,128)(2,1)S(1)}, bf16[400,256]{1,0:T(8,128)(2,1)S(1)}, u32[]{:S(2)}, u32[]{:S(2)}) %collective-permute-start.3) | collective-permute-done | bytes 204832 | tf_op jit(solution)/shard_map/ppermute | solution.py:34
  20.2 0.3 merge.1.a_ref
  20.6 0.0 collective-permute-done.4.refs_2_
  20.6 0.0 collective-permute-done.5.refs_5_
  20.6 0.6 collective-permute-start.6
  21.2 0.0 collective-permute-start.8
  21.2 3.2 %collective-permute-start.9 = (bf16[128,2304]{1,0:T(8,128)(2,1)S(1)}, bf16[128,2304]{1,0:T(8,128)(2,1)S(1)}, u32[]{:S(2)}, u32[]{:S(2)}) collective-permute-start(bf16[128,2304]{1,0:T(8,128)(2,1)S(1)} %get-tuple-element.20.refs_0_), channel_id=1, source_target_pairs={{0,24},{8,0},{16,8},{24,16},{1,25},{9,1},{17,9},{25,17},{2,26},{10... | collective-permute-start | bytes 1769480 | tf_op jit(solution)/shard_map/ppermute | solution.py:339
  24.5 0.0 collective-permute-start.10
  24.5 3.2 %collective-permute-start.11 = (bf16[128,2304]{1,0:T(8,128)(2,1)S(1)}, bf16[128,2304]{1,0:T(8,128)(2,1)S(1)}, u32[]{:S(2)}, u32[]{:S(2)}) collective-permute-start(bf16[128,2304]{1,0:T(8,128)(2,1)S(1)} %collective-permute-done.5.refs_5_), channel_id=1, source_target_pairs={{0,24},{8,0},{16,8},{24,16},{1,25},{9,1},{17,9},{25,17},{2,26},{10... | collective-permute-start | bytes 1769480 | tf_op jit(solution)/shard_map/ppermute | solution.py:339
  27.7 0.3 collective-permute-done.6.b_ref
  28.0 0.6 finish.1
  28.6 21.1 %all_to_all.10 = bf16[16,24,256]{2,1,0:T(8,128)(2,1)S(1)} all-to-all(bf16[16,24,256]{2,1,0:T(8,128)(2,1)S(1)} %bitcast.8), channel_id=1, replica_groups=mesh['z'=8,'x'=4,'yh'=2,'yl'=2,'core'=2] {'z','yh'}, dimensions={0} | all-to-all | bytes 393216 | tf_op jit(solution)/shard_map/all_to_all | solution.py:365
  49.7 0.0 collective-permute-start.7
  49.7 0.0 collective-permute-done.8.refs_3_
  49.7 0.0 collective-permute-done.9.refs_4_
  49.7 1.4 %collective-permute-done.7.theirs_ref = bf16[384,256]{1,0:T(8,128)(2,1)S(1)} collective-permute-done((bf16[384,256]{1,0:T(8,128)(2,1)S(1)}, bf16[384,256]{1,0:T(8,128)(2,1)S(1)}, u32[]{:S(2)}, u32[]{:S(2)}) %collective-permute-start.7) | collective-permute-done | bytes 196640 | tf_op jit(solution)/shard_map/ppermute | solution.py:34
  51.1 1.9 %project_near.1 = (f32[64,1792]{1,0:T(8,128)S(1)}, bf16[128,512]{1,0:T(8,128)(2,1)S(1)}) custom-call(s32[3]{0:T(128)S(1)} %pad_add_fusion.place_ref, bf16[384,256]{1,0:T(8,128)(2,1)S(1)} %bitcast.7, bf16[384,256]{1,0:T(8,128)(2,1)S(1)} %collective-permute-done.7.theirs_ref, bf16[128,2304]{1,0:T(8,128)(2,1)S(1)} %get-tuple-element.20.refs_0_, ...), custom_call_target="tpu_custom_call" | custom-call | tf_op jit(solution)/shard_map/project_near/pallas_call | solution.py:295
  53.0 0.0 collective-permute-done.10.refs_0_
  53.0 0.0 collective-permute-done.11.refs_1_
  53.0 0.4 project_far.1
  53.5 19.2 %all_to_all.11.part_ref = bf16[16,3,1792]{2,1,0:T(4,128)(2,1)S(1)} all-to-all(bf16[16,3,1792]{2,1,0:T(4,128)(2,1)S(1)} %project_far.1), channel_id=1, replica_groups=mesh['z'=8,'x'=4,'yh'=2,'yl'=2,'core'=2] {'z','yh'}, dimensions={0} | all-to-all | bytes 344064 | tf_op jit(solution)/shard_map/all_to_all | solution.py:371
  72.6 0.6 total.1
Async XLA Ops:
  0.0 12.7 %copy-start = (s32[3]{0:T(128)S(1)}, s32[3]{0:T(128)}, u32[]{:S(2)}) copy-start(s32[3]{0:T(128)} %length_ref.1) | copy-start | bytes 40
  1.3 19.2 %collective-permute-start.4 = (bf16[128,2304]{1,0:T(8,128)(2,1)S(1)}, bf16[128,2304]{1,0:T(8,128)(2,1)S(1)}, u32[]{:S(2)}, u32[]{:S(2)}) collective-permute-start(bf16[128,2304]{1,0:T(8,128)(2,1)S(1)} %get-tuple-element.20.refs_0_), channel_id=1, source_target_pairs={{0,8},{8,16},{16,24},{24,0},{1,9},{9,17},{17,25},{25,1},{2,10},{10... | collective-permute-start | bytes 1769480 | tf_op jit(solution)/shard_map/ppermute | solution.py:339
  2.9 17.7 %collective-permute-start.5 = (bf16[128,2304]{1,0:T(8,128)(2,1)S(1)}, bf16[128,2304]{1,0:T(8,128)(2,1)S(1)}, u32[]{:S(2)}, u32[]{:S(2)}) collective-permute-start(bf16[128,2304]{1,0:T(8,128)(2,1)S(1)} %get-tuple-element.21.refs_1_), channel_id=1, source_target_pairs={{0,24},{8,0},{16,8},{24,16},{1,25},{9,1},{17,9},{25,17},{2,26},{10... | collective-permute-start | bytes 1769480 | tf_op jit(solution)/shard_map/ppermute | solution.py:339
  4.7 6.5 %collective-permute-start.1 = (bf16[3,32,576]{2,1,0:T(8,128)(2,1)}, bf16[3,32,576]{2,1,0:T(8,128)(2,1)S(1)}, u32[]{:S(2)}, u32[]{:S(2)}) collective-permute-start(bf16[3,32,576]{2,1,0:T(8,128)(2,1)} %query_ref.1), channel_id=1, source_target_pairs={{0,2},{2,0},{1,3},{3,1},{4,6},{6,4},{5,7},{7,5},{8,10},{10,8},{9,1... | collective-permute-start | bytes 331784 | tf_op jit(solution)/shard_map/ppermute | solution.py:34
  6.8 5.0 %collective-permute-start = (bf16[3,32,576]{2,1,0:T(8,128)(2,1)}, bf16[3,32,576]{2,1,0:T(8,128)(2,1)S(1)}, u32[]{:S(2)}, u32[]{:S(2)}) collective-permute-start(bf16[3,32,576]{2,1,0:T(8,128)(2,1)} %query_ref.1), channel_id=1, source_target_pairs={{0,1},{1,0},{2,3},{3,2},{4,5},{5,4},{6,7},{7,6},{8,9},{9,8},{10,11... | collective-permute-start | bytes 331784 | tf_op jit(solution)/shard_map/ppermute | solution.py:34
  11.2 1.6 %collective-permute-start.2 = (bf16[3,32,576]{2,1,0:T(8,128)(2,1)S(1)}, bf16[3,32,576]{2,1,0:T(8,128)(2,1)S(1)}, u32[]{:S(2)}, u32[]{:S(2)}) collective-permute-start(bf16[3,32,576]{2,1,0:T(8,128)(2,1)S(1)} %collective-permute-done.1.refs_2_), channel_id=1, source_target_pairs={{0,1},{1,0},{2,3},{3,2},{4,5},{5,4},{6,7},{7,6},{8,9},{9,8},{10,11... | collective-permute-start | bytes 331784 | tf_op jit(solution)/shard_map/ppermute | solution.py:34
  18.7 1.5 %collective-permute-start.3 = (bf16[400,256]{1,0:T(8,128)(2,1)S(1)}, bf16[400,256]{1,0:T(8,128)(2,1)S(1)}, u32[]{:S(2)}, u32[]{:S(2)}) collective-permute-start(bf16[400,256]{1,0:T(8,128)(2,1)S(1)} %get-tuple-element.19), channel_id=1, source_target_pairs={{0,1},{1,0},{2,3},{3,2},{4,5},{5,4},{6,7},{7,6},{8,9},{9,8},{10,11... | collective-permute-start | bytes 614408 | tf_op jit(solution)/shard_map/ppermute | solution.py:34
  20.6 7.4 %collective-permute-start.6 = (bf16[400,256]{1,0:T(8,128)(2,1)S(1)}, bf16[400,256]{1,0:T(8,128)(2,1)S(1)}, u32[]{:S(2)}, u32[]{:S(2)}) collective-permute-start(bf16[400,256]{1,0:T(8,128)(2,1)S(1)} %merge.1.a_ref), channel_id=1, source_target_pairs={{0,2},{2,0},{1,3},{3,1},{4,6},{6,4},{5,7},{7,5},{8,10},{10,8},{9,1... | collective-permute-start | bytes 614408 | tf_op jit(solution)/shard_map/ppermute | solution.py:34
  21.2 28.4 %collective-permute-start.8 = (bf16[128,2304]{1,0:T(8,128)(2,1)S(1)}, bf16[128,2304]{1,0:T(8,128)(2,1)S(1)}, u32[]{:S(2)}, u32[]{:S(2)}) collective-permute-start(bf16[128,2304]{1,0:T(8,128)(2,1)S(1)} %get-tuple-element.21.refs_1_), channel_id=1, source_target_pairs={{0,8},{8,16},{16,24},{24,0},{1,9},{9,17},{17,25},{25,1},{2,10},{10... | collective-permute-start | bytes 1769480 | tf_op jit(solution)/shard_map/ppermute | solution.py:339
  21.2 28.4 %collective-permute-start.9 = (bf16[128,2304]{1,0:T(8,128)(2,1)S(1)}, bf16[128,2304]{1,0:T(8,128)(2,1)S(1)}, u32[]{:S(2)}, u32[]{:S(2)}) collective-permute-start(bf16[128,2304]{1,0:T(8,128)(2,1)S(1)} %get-tuple-element.20.refs_0_), channel_id=1, source_target_pairs={{0,24},{8,0},{16,8},{24,16},{1,25},{9,1},{17,9},{25,17},{2,26},{10... | collective-permute-start | bytes 1769480 | tf_op jit(solution)/shard_map/ppermute | solution.py:339
  24.5 28.6 %collective-permute-start.10 = (bf16[128,2304]{1,0:T(8,128)(2,1)S(1)}, bf16[128,2304]{1,0:T(8,128)(2,1)S(1)}, u32[]{:S(2)}, u32[]{:S(2)}) collective-permute-start(bf16[128,2304]{1,0:T(8,128)(2,1)S(1)} %collective-permute-done.4.refs_2_), channel_id=1, source_target_pairs={{0,8},{8,16},{16,24},{24,0},{1,9},{9,17},{17,25},{25,1},{2,10},{10... | collective-permute-start | bytes 1769480 | tf_op jit(solution)/shard_map/ppermute | solution.py:339
  24.5 28.6 %collective-permute-start.11 = (bf16[128,2304]{1,0:T(8,128)(2,1)S(1)}, bf16[128,2304]{1,0:T(8,128)(2,1)S(1)}, u32[]{:S(2)}, u32[]{:S(2)}) collective-permute-start(bf16[128,2304]{1,0:T(8,128)(2,1)S(1)} %collective-permute-done.5.refs_5_), channel_id=1, source_target_pairs={{0,24},{8,0},{16,8},{24,16},{1,25},{9,1},{17,9},{25,17},{2,26},{10... | collective-permute-start | bytes 1769480 | tf_op jit(solution)/shard_map/ppermute | solution.py:339
  49.7 1.4 %collective-permute-start.7 = (bf16[384,256]{1,0:T(8,128)(2,1)S(1)}, bf16[384,256]{1,0:T(8,128)(2,1)S(1)}, u32[]{:S(2)}, u32[]{:S(2)}) collective-permute-start(bf16[384,256]{1,0:T(8,128)(2,1)S(1)} %bitcast.6), channel_id=1, source_target_pairs={{0,1},{1,0},{2,3},{3,2},{4,5},{5,4},{6,7},{7,6},{8,9},{9,8},{10,11... | collective-permute-start | bytes 589832 | tf_op jit(solution)/shard_map/ppermute | solution.py:34

commit v5 on v4

--- a/solution.py
+++ b/solution.py
@@ -356,8 +356,8 @@
     query_parts = [held, partner, across, swap(across, "core")]
     mine, theirs = attend(places, lengths, query_parts, cache, lat)
     behind_too, ahead_too = from_x(own[1], 1), from_x(own[0], -1)
+    theirs, behind, ahead = lax.optimization_barrier((theirs, behind, ahead))
     state = merge(mine, swap(theirs, "core"), rows, heads)
-    state, behind, ahead = lax.optimization_barrier((state, behind, ahead))
     tiles = [*own, behind, behind_too, ahead_too, ahead, from_x(behind, 1), from_x(ahead, -1)]
     latents = finish(state, swap(state, "yl"), rows, heads, owned, sizes)
 

time: 74.3 us -> 74.4 us (level)
  transfers between devices with their start and end apart: 12 -> 12, of which waited for: 4 -> 4; matrix products, arithmetic and copies ran while one was open for 0% -> 0% of each run, Pallas kernels for 18% -> 17%
where the time goes in v5:
time: 74.4 us; the launch traced here: 73.3 us
  blocking collectives  40.2 us (54%)
  Pallas kernels  15.5 us (21%)
  starting transfers between devices  13.7 us (18%)
  waiting for transfers between devices  3.76 us (5%)
    all_to_all x1, blocking collectives, shards(): latents = lax.all_to_all(latents, PEERS, 0, 0, tiled=True)  21 us
    all_to_all x1, blocking collectives, shards(): partial = lax.all_to_all(partial, PEERS, 0, 0, tiled=True)  19.2 us
    ppermute x6, starting transfers between devices, from_x(): lax.ppermute(block, 'x', [(i, (i + distance) % size) for i in range(size)])  9.79 us
    pallas_call x1, Pallas kernels, attend(): call(functools.partial(attend_kernel, lat), 'attend', [shape, shape], [SM...  5.94 us
    pallas_call x1, Pallas kernels, load(): call(load_kernel, 'load', [pltpu.VMEM(cache.shape, cache.dtype), pltpu.VM...  4.31 us
    ppermute x6, starting transfers between devices, swap(): return lax.ppermute(block, axis, [(0, 1), (1, 0)])  3.88 us
    ppermute x6, waiting for transfers between devices, swap(): return lax.ppermute(block, axis, [(0, 1), (1, 0)])  3.74 us
    pallas_call x1, Pallas kernels, project_near(): call(functools.partial(near_kernel, rows, owned, width), 'project_near',...  1.91 us
  transfers between devices with their start and end apart: 12, of which 4 were waited for; matrix products, arithmetic and copies ran while one was open for 0% of the time, Pallas kernels for 17%

profile of v5, /device:TPU:8, one launch (start us, length us, event | category | flops | bytes accessed | tf_op | source)
XLA Modules:
  0.0 73.3 jit_solution(10445960950005226807)
XLA Ops:
  0.0 0.0 copy-start
  0.0 1.3 %pack.1 = (bf16[128,2304]{1,0:T(8,128)(2,1)S(1)}, bf16[128,2304]{1,0:T(8,128)(2,1)S(1)}) custom-call(bf16[2,512,128]{2,1,0:T(8,128)(2,1)} %up_ref.1, bf16[256,1792]{1,0:T(8,128)(2,1)} %weight_ref.1), custom_call_target="tpu_custom_call" | custom-call | tf_op jit(solution)/shard_map/pack/pallas_call | solution.py:78
  1.3 1.6 %collective-permute-start.3 = (bf16[128,2304]{1,0:T(8,128)(2,1)S(1)}, bf16[128,2304]{1,0:T(8,128)(2,1)S(1)}, u32[]{:S(2)}, u32[]{:S(2)}) collective-permute-start(bf16[128,2304]{1,0:T(8,128)(2,1)S(1)} %get-tuple-element.20.refs_0_), channel_id=1, source_target_pairs={{0,8},{8,16},{16,24},{24,0},{1,9},{9,17},{17,25},{25,1},{2,10},{10... | collective-permute-start | bytes 1769480 | tf_op jit(solution)/shard_map/ppermute | solution.py:339
  2.9 1.7 %collective-permute-start.4 = (bf16[128,2304]{1,0:T(8,128)(2,1)S(1)}, bf16[128,2304]{1,0:T(8,128)(2,1)S(1)}, u32[]{:S(2)}, u32[]{:S(2)}) collective-permute-start(bf16[128,2304]{1,0:T(8,128)(2,1)S(1)} %get-tuple-element.21.refs_1_), channel_id=1, source_target_pairs={{0,24},{8,0},{16,8},{24,16},{1,25},{9,1},{17,9},{25,17},{2,26},{10... | collective-permute-start | bytes 1769480 | tf_op jit(solution)/shard_map/ppermute | solution.py:339
  4.7 2.2 %collective-permute-start.1 = (bf16[3,32,576]{2,1,0:T(8,128)(2,1)}, bf16[3,32,576]{2,1,0:T(8,128)(2,1)S(1)}, u32[]{:S(2)}, u32[]{:S(2)}) collective-permute-start(bf16[3,32,576]{2,1,0:T(8,128)(2,1)} %query_ref.1), channel_id=1, source_target_pairs={{0,2},{2,0},{1,3},{3,1},{4,6},{6,4},{5,7},{7,5},{8,10},{10,8},{9,1... | collective-permute-start | bytes 331784 | tf_op jit(solution)/shard_map/ppermute | solution.py:34
  6.8 0.0 collective-permute-start
  6.8 4.3 %load.1 = (bf16[3,576,3200]{2,1,0:T(8,128)(2,1)S(1)}, bf16[3,32,576]{2,1,0:T(8,128)(2,1)S(1)}) custom-call(bf16[3,576,3200]{2,1,0:T(8,128)(2,1)} %bitcast.9, bf16[3,32,576]{2,1,0:T(8,128)(2,1)} %query_ref.1), custom_call_target="tpu_custom_call" | custom-call | flops 12582912 | bytes 12582912 | tf_op jit(solution)/shard_map/load/pallas_call | solution.py:100
  11.2 0.0 collective-permute-done.1.refs_2_
  11.2 0.6 collective-permute-start.2
  11.8 0.1 pad_add_fusion.place_ref
  11.8 0.0 collective-permute-done.refs_1_
  11.8 0.9 %collective-permute-done.2.refs_3_ = bf16[3,32,576]{2,1,0:T(8,128)(2,1)S(1)} collective-permute-done((bf16[3,32,576]{2,1,0:T(8,128)(2,1)S(1)}, bf16[3,32,576]{2,1,0:T(8,128)(2,1)S(1)}, u32[]{:S(2)}, u32[]{:S(2)}) %collective-permute-start.2) | collective-permute-done | bytes 110624 | tf_op jit(solution)/shard_map/ppermute | solution.py:34
  12.7 0.0 copy-done
  12.7 5.9 %attend.1 = (bf16[400,256]{1,0:T(8,128)(2,1)S(1)}, bf16[400,256]{1,0:T(8,128)(2,1)S(1)}) custom-call(s32[3]{0:T(128)S(1)} %pad_add_fusion.place_ref, s32[3]{0:T(128)S(1)} %copy-done, bf16[3,32,576]{2,1,0:T(8,128)(2,1)S(1)} %get-tuple-element.16.refs_0_, bf16[3,32,576]{2,1,0:T(8,128)(2,1)S(1)} %collective-permute-done.refs_1_, ...), custom_call_target="tpu_custom_call" | custom-call | tf_op jit(solution)/shard_map/attend/pallas_call | solution.py:179
  18.7 0.0 collective-permute-done.3.refs_2_
  18.7 0.0 collective-permute-done.4.refs_5_
  18.7 0.5 collective-permute-start.5
  19.2 1.1 %collective-permute-done.5.b_ref = bf16[400,256]{1,0:T(8,128)(2,1)S(1)} collective-permute-done((bf16[400,256]{1,0:T(8,128)(2,1)S(1)}, bf16[400,256]{1,0:T(8,128)(2,1)S(1)}, u32[]{:S(2)}, u32[]{:S(2)}) %collective-permute-start.5) | collective-permute-done | bytes 204832 | tf_op jit(solution)/shard_map/ppermute | solution.py:34
  20.3 0.3 merge.1.a_ref
  20.6 0.6 collective-permute-start.6
  21.2 0.3 collective-permute-start.8
  21.5 3.0 %collective-permute-start.9 = (bf16[128,2304]{1,0:T(8,128)(2,1)S(1)}, bf16[128,2304]{1,0:T(8,128)(2,1)S(1)}, u32[]{:S(2)}, u32[]{:S(2)}) collective-permute-start(bf16[128,2304]{1,0:T(8,128)(2,1)S(1)} %get-tuple-element.20.refs_0_), channel_id=1, source_target_pairs={{0,24},{8,0},{16,8},{24,16},{1,25},{9,1},{17,9},{25,17},{2,26},{10... | collective-permute-start | bytes 1769480 | tf_op jit(solution)/shard_map/ppermute | solution.py:339
  24.5 0.0 collective-permute-start.10
  24.5 3.2 %collective-permute-start.11 = (bf16[128,2304]{1,0:T(8,128)(2,1)S(1)}, bf16[128,2304]{1,0:T(8,128)(2,1)S(1)}, u32[]{:S(2)}, u32[]{:S(2)}) collective-permute-start(bf16[128,2304]{1,0:T(8,128)(2,1)S(1)} %collective-permute-done.4.refs_5_), channel_id=1, source_target_pairs={{0,24},{8,0},{16,8},{24,16},{1,25},{9,1},{17,9},{25,17},{2,26},{10... | collective-permute-start | bytes 1769480 | tf_op jit(solution)/shard_map/ppermute | solution.py:339
  27.7 0.3 collective-permute-done.6.b_ref
  28.0 0.6 finish.1
  28.6 21.0 %all_to_all.10 = bf16[16,24,256]{2,1,0:T(8,128)(2,1)S(1)} all-to-all(bf16[16,24,256]{2,1,0:T(8,128)(2,1)S(1)} %bitcast.8), channel_id=1, replica_groups=mesh['z'=8,'x'=4,'yh'=2,'yl'=2,'core'=2] {'z','yh'}, dimensions={0} | all-to-all | bytes 393216 | tf_op jit(solution)/shard_map/all_to_all | solution.py:365
  49.6 0.0 collective-permute-start.7
  49.6 0.0 collective-permute-done.8.refs_3_
  49.6 0.0 collective-permute-done.9.refs_4_
  49.6 1.4 %collective-permute-done.7.theirs_ref = bf16[384,256]{1,0:T(8,128)(2,1)S(1)} collective-permute-done((bf16[384,256]{1,0:T(8,128)(2,1)S(1)}, bf16[384,256]{1,0:T(8,128)(2,1)S(1)}, u32[]{:S(2)}, u32[]{:S(2)}) %collective-permute-start.7) | collective-permute-done | bytes 196640 | tf_op jit(solution)/shard_map/ppermute | solution.py:34
  51.1 1.9 %project_near.1 = (f32[64,1792]{1,0:T(8,128)S(1)}, bf16[128,512]{1,0:T(8,128)(2,1)S(1)}) custom-call(s32[3]{0:T(128)S(1)} %pad_add_fusion.place_ref, bf16[384,256]{1,0:T(8,128)(2,1)S(1)} %bitcast.7, bf16[384,256]{1,0:T(8,128)(2,1)S(1)} %collective-permute-done.7.theirs_ref, bf16[128,2304]{1,0:T(8,128)(2,1)S(1)} %get-tuple-element.20.refs_0_, ...), custom_call_target="tpu_custom_call" | custom-call | tf_op jit(solution)/shard_map/project_near/pallas_call | solution.py:295
  53.0 0.0 collective-permute-done.10.refs_0_
  53.0 0.0 collective-permute-done.11.refs_1_
  53.0 0.4 project_far.1
  53.5 19.2 %all_to_all.11.part_ref = bf16[16,3,1792]{2,1,0:T(4,128)(2,1)S(1)} all-to-all(bf16[16,3,1792]{2,1,0:T(4,128)(2,1)S(1)} %project_far.1), channel_id=1, replica_groups=mesh['z'=8,'x'=4,'yh'=2,'yl'=2,'core'=2] {'z','yh'}, dimensions={0} | all-to-all | bytes 344064 | tf_op jit(solution)/shard_map/all_to_all | solution.py:371
  72.6 0.6 total.1
Async XLA Ops:
  0.0 12.7 %copy-start = (s32[3]{0:T(128)S(1)}, s32[3]{0:T(128)}, u32[]{:S(2)}) copy-start(s32[3]{0:T(128)} %length_ref.1) | copy-start | bytes 40
  1.3 17.4 %collective-permute-start.3 = (bf16[128,2304]{1,0:T(8,128)(2,1)S(1)}, bf16[128,2304]{1,0:T(8,128)(2,1)S(1)}, u32[]{:S(2)}, u32[]{:S(2)}) collective-permute-start(bf16[128,2304]{1,0:T(8,128)(2,1)S(1)} %get-tuple-element.20.refs_0_), channel_id=1, source_target_pairs={{0,8},{8,16},{16,24},{24,0},{1,9},{9,17},{17,25},{25,1},{2,10},{10... | collective-permute-start | bytes 1769480 | tf_op jit(solution)/shard_map/ppermute | solution.py:339
  2.9 15.8 %collective-permute-start.4 = (bf16[128,2304]{1,0:T(8,128)(2,1)S(1)}, bf16[128,2304]{1,0:T(8,128)(2,1)S(1)}, u32[]{:S(2)}, u32[]{:S(2)}) collective-permute-start(bf16[128,2304]{1,0:T(8,128)(2,1)S(1)} %get-tuple-element.21.refs_1_), channel_id=1, source_target_pairs={{0,24},{8,0},{16,8},{24,16},{1,25},{9,1},{17,9},{25,17},{2,26},{10... | collective-permute-start | bytes 1769480 | tf_op jit(solution)/shard_map/ppermute | solution.py:339
  4.7 6.5 %collective-permute-start.1 = (bf16[3,32,576]{2,1,0:T(8,128)(2,1)}, bf16[3,32,576]{2,1,0:T(8,128)(2,1)S(1)}, u32[]{:S(2)}, u32[]{:S(2)}) collective-permute-start(bf16[3,32,576]{2,1,0:T(8,128)(2,1)} %query_ref.1), channel_id=1, source_target_pairs={{0,2},{2,0},{1,3},{3,1},{4,6},{6,4},{5,7},{7,5},{8,10},{10,8},{9,1... | collective-permute-start | bytes 331784 | tf_op jit(solution)/shard_map/ppermute | solution.py:34
  6.8 5.0 %collective-permute-start = (bf16[3,32,576]{2,1,0:T(8,128)(2,1)}, bf16[3,32,576]{2,1,0:T(8,128)(2,1)S(1)}, u32[]{:S(2)}, u32[]{:S(2)}) collective-permute-start(bf16[3,32,576]{2,1,0:T(8,128)(2,1)} %query_ref.1), channel_id=1, source_target_pairs={{0,1},{1,0},{2,3},{3,2},{4,5},{5,4},{6,7},{7,6},{8,9},{9,8},{10,11... | collective-permute-start | bytes 331784 | tf_op jit(solution)/shard_map/ppermute | solution.py:34
  11.2 1.6 %collective-permute-start.2 = (bf16[3,32,576]{2,1,0:T(8,128)(2,1)S(1)}, bf16[3,32,576]{2,1,0:T(8,128)(2,1)S(1)}, u32[]{:S(2)}, u32[]{:S(2)}) collective-permute-start(bf16[3,32,576]{2,1,0:T(8,128)(2,1)S(1)} %collective-permute-done.1.refs_2_), channel_id=1, source_target_pairs={{0,1},{1,0},{2,3},{3,2},{4,5},{5,4},{6,7},{7,6},{8,9},{9,8},{10,11... | collective-permute-start | bytes 331784 | tf_op jit(solution)/shard_map/ppermute | solution.py:34
  18.7 1.5 %collective-permute-start.5 = (bf16[400,256]{1,0:T(8,128)(2,1)S(1)}, bf16[400,256]{1,0:T(8,128)(2,1)S(1)}, u32[]{:S(2)}, u32[]{:S(2)}) collective-permute-start(bf16[400,256]{1,0:T(8,128)(2,1)S(1)} %get-tuple-element.22), channel_id=1, source_target_pairs={{0,1},{1,0},{2,3},{3,2},{4,5},{5,4},{6,7},{7,6},{8,9},{9,8},{10,11... | collective-permute-start | bytes 614408 | tf_op jit(solution)/shard_map/ppermute | solution.py:34
  20.6 7.4 %collective-permute-start.6 = (bf16[400,256]{1,0:T(8,128)(2,1)S(1)}, bf16[400,256]{1,0:T(8,128)(2,1)S(1)}, u32[]{:S(2)}, u32[]{:S(2)}) collective-permute-start(bf16[400,256]{1,0:T(8,128)(2,1)S(1)} %merge.1.a_ref), channel_id=1, source_target_pairs={{0,2},{2,0},{1,3},{3,1},{4,6},{6,4},{5,7},{7,5},{8,10},{10,8},{9,1... | collective-permute-start | bytes 614408 | tf_op jit(solution)/shard_map/ppermute | solution.py:34
  21.2 28.4 %collective-permute-start.8 = (bf16[128,2304]{1,0:T(8,128)(2,1)S(1)}, bf16[128,2304]{1,0:T(8,128)(2,1)S(1)}, u32[]{:S(2)}, u32[]{:S(2)}) collective-permute-start(bf16[128,2304]{1,0:T(8,128)(2,1)S(1)} %get-tuple-element.21.refs_1_), channel_id=1, source_target_pairs={{0,8},{8,16},{16,24},{24,0},{1,9},{9,17},{17,25},{25,1},{2,10},{10... | collective-permute-start | bytes 1769480 | tf_op jit(solution)/shard_map/ppermute | solution.py:339
  21.5 28.1 %collective-permute-start.9 = (bf16[128,2304]{1,0:T(8,128)(2,1)S(1)}, bf16[128,2304]{1,0:T(8,128)(2,1)S(1)}, u32[]{:S(2)}, u32[]{:S(2)}) collective-permute-start(bf16[128,2304]{1,0:T(8,128)(2,1)S(1)} %get-tuple-element.20.refs_0_), channel_id=1, source_target_pairs={{0,24},{8,0},{16,8},{24,16},{1,25},{9,1},{17,9},{25,17},{2,26},{10... | collective-permute-start | bytes 1769480 | tf_op jit(solution)/shard_map/ppermute | solution.py:339
  24.5 28.5 %collective-permute-start.10 = (bf16[128,2304]{1,0:T(8,128)(2,1)S(1)}, bf16[128,2304]{1,0:T(8,128)(2,1)S(1)}, u32[]{:S(2)}, u32[]{:S(2)}) collective-permute-start(bf16[128,2304]{1,0:T(8,128)(2,1)S(1)} %collective-permute-done.3.refs_2_), channel_id=1, source_target_pairs={{0,8},{8,16},{16,24},{24,0},{1,9},{9,17},{17,25},{25,1},{2,10},{10... | collective-permute-start | bytes 1769480 | tf_op jit(solution)/shard_map/ppermute | solution.py:339
  24.5 28.6 %collective-permute-start.11 = (bf16[128,2304]{1,0:T(8,128)(2,1)S(1)}, bf16[128,2304]{1,0:T(8,128)(2,1)S(1)}, u32[]{:S(2)}, u32[]{:S(2)}) collective-permute-start(bf16[128,2304]{1,0:T(8,128)(2,1)S(1)} %collective-permute-done.4.refs_5_), channel_id=1, source_target_pairs={{0,24},{8,0},{16,8},{24,16},{1,25},{9,1},{17,9},{25,17},{2,26},{10... | collective-permute-start | bytes 1769480 | tf_op jit(solution)/shard_map/ppermute | solution.py:339
  49.6 1.4 %collective-permute-start.7 = (bf16[384,256]{1,0:T(8,128)(2,1)S(1)}, bf16[384,256]{1,0:T(8,128)(2,1)S(1)}, u32[]{:S(2)}, u32[]{:S(2)}) collective-permute-start(bf16[384,256]{1,0:T(8,128)(2,1)S(1)} %bitcast.6), channel_id=1, source_target_pairs={{0,1},{1,0},{2,3},{3,2},{4,5},{5,4},{6,7},{7,6},{8,9},{9,8},{10,11... | collective-permute-start | bytes 589832 | tf_op jit(solution)/shard_map/ppermute | solution.py:34
